TPU v7x, 32 devices: a whole 2x2x4 slice. The times are simulated.
32 devices in a mesh: turb: 2 (over x), age: 4 (over z), span: 4 (over y, core).
Axes of the slice: x: 2, y: 2, z: 4, core: 2. Of those that a mesh axis runs over, the one named last changes fastest.
Arguments:
- positions: float32 [3, 4, 3, 64, 512], P(None, 'turb', None, 'span', 'age'), may hold values from -6 to 6
- strengths: float32 [2, 4, 3, 64, 512], P(None, 'turb', None, 'span', 'age'), may hold values from -12 to 12
- core_radius: float32 [4, 3, 64, 512], P('turb', None, 'span', 'age'), may hold values from 0.3 to 1.5
- adjoint_seed: float32 [3, 4, 3, 64, 512], P(None, 'turb', None, 'span', 'age'), may hold values from -6 to 6
- pair_target: int32 [2, 4, 4, 128], P('turb', 'age', 'span'), may hold values from 0 to 95
- pair_owner: int32 [2, 4, 4, 128], P('turb', 'age', 'span'), may hold values from 0 to 7, as said below
- pair_source: int32 [2, 4, 4, 128], P('turb', 'age', 'span'), may hold values from 0 to 95
Outputs:
- advected: float32 [3, 4, 3, 64, 512], P(None, 'turb', None, 'span', 'age')
- grad_positions: float32 [3, 4, 3, 64, 512], P(None, 'turb', None, 'span', 'age')
- grad_strengths: float32 [2, 4, 3, 64, 512], P(None, 'turb', None, 'span', 'age')
Inputs may be any that keep to these rules, and one draw needn't show every extreme that they name: `pair_owner`: at most 32 of the pairs of one device name one owner. One owner, the same for all devices, is named by exactly 32 pairs of every device.
All inputs are finite; a program needn't handle non-finite values.
Results may differ from a plain program's by a relative error of at most 0.0003.
Values sent between devices are 32-bit elements; how exact they have to be, the bound alone decides.
A program may use at most 64 MiB of HBM per device.

v0:
```python
import math

import jax
import jax.numpy as jnp
from jax import lax
from jax.sharding import PartitionSpec as P

REACH = 8


time_step = 0.5
four_pi = 4.0 * math.pi
batch_rows = 16


def shifted_2(value, axis, steps):
    count = lax.axis_size(axis)
    leading, last = (max(0, -steps), min(count, count - steps))
    return lax.ppermute(value, axis, [(source, source + steps) for source in range(leading, last)])


def windows(payload):
    age_count = payload.shape[-1]
    padded = jnp.pad(payload, ((0, 0), (0, 0), (REACH, REACH)))
    stacked = jnp.stack(
        [
            padded[:, :, REACH + offset : REACH + offset + age_count]
            for offset in range(-REACH, REACH)
        ]
    )
    shifted = (
        jnp.arange(-REACH, REACH, dtype=jnp.int32)[:, None]
        + jnp.arange(age_count, dtype=jnp.int32)[None, :]
    )
    inside = ((shifted >= 0) & (shifted < age_count)).astype(payload.dtype)
    return (stacked, inside)


def induced(targets, payload):
    stacked, inside = windows(payload)
    begins = stacked[:, :, 0:3]
    end_points = jnp.stack([stacked[:, :, 3:6], stacked[:, :, 6:9]])
    gammas = jnp.stack([stacked[:, :, 9], stacked[:, :, 10]]) * inside[None, :, None, :]
    core = jnp.where(inside[:, None, :] > 0, stacked[:, :, 11], 1.0)
    core_sq = core * core
    core_quad = core_sq * core_sq
    from_begin = targets[None] - begins
    from_end = targets[None, None] - end_points
    along = end_points - begins[None]
    near = from_begin[None]
    cross_x = near[..., 1, :] * from_end[..., 2, :] - near[..., 2, :] * from_end[..., 1, :]
    cross_y = near[..., 2, :] * from_end[..., 0, :] - near[..., 0, :] * from_end[..., 2, :]
    cross_z = near[..., 0, :] * from_end[..., 1, :] - near[..., 1, :] * from_end[..., 0, :]
    cross_sq = cross_x * cross_x + cross_y * cross_y + cross_z * cross_z
    length_sq = jnp.sum(along * along, axis=-2) + core_sq
    dist_begin = jnp.sqrt(jnp.sum(from_begin * from_begin, axis=-2) + core_sq)
    dist_end = jnp.sqrt(jnp.sum(from_end * from_end, axis=-2) + core_sq)
    projected = jnp.sum(
        along * (near / dist_begin[None, :, :, None, :] - from_end / dist_end[..., None, :]),
        axis=-2,
    )
    factor = (
        gammas
        * projected
        / (four_pi * jnp.sqrt(cross_sq * cross_sq + core_quad * length_sq * length_sq))
    )
    return jnp.stack(
        [
            jnp.sum(cross_x * factor, axis=(0, 1)),
            jnp.sum(cross_y * factor, axis=(0, 1)),
            jnp.sum(cross_z * factor, axis=(0, 1)),
        ],
        axis=1,
    )


def run_pairs(targets, payload, cotangent):
    number = targets.shape[0]
    age_count = targets.shape[-1]

    def one_batch(operands):
        velocity, pullback = jax.vjp(induced, operands[0], operands[1])
        grad_targets, grad_payload = pullback(operands[2])
        return (velocity, grad_targets, grad_payload)

    shaped = (
        targets.reshape(number // batch_rows, batch_rows, 3, age_count),
        payload.reshape(number // batch_rows, batch_rows, 12, age_count),
        cotangent.reshape(number // batch_rows, batch_rows, 3, age_count),
    )
    velocity, grad_targets, grad_payload = lax.map(one_batch, shaped)
    return (
        velocity.reshape(number, 3, age_count),
        grad_targets.reshape(number, 3, age_count),
        grad_payload.reshape(number, 12, age_count),
    )


def onehot_sum(indices, rows, values):
    selector = (jnp.arange(rows, dtype=jnp.int32)[:, None] == indices[None, :]).astype(jnp.float32)
    flat = values.reshape(values.shape[0], -1)
    summed = jnp.dot(
        selector, flat, precision=lax.Precision.HIGHEST, preferred_element_type=jnp.float32
    )
    return summed.reshape((rows,) + values.shape[1:])


def local(positions, strengths, core_radius, adjoint_seed, pair_target, pair_owner, pair_source):
    shape_here = positions.shape
    station_here = shape_here[3]
    age_here = shape_here[4]
    blocks_here = shape_here[1] * shape_here[2] * station_here
    group_size = lax.axis_size("turb") * lax.axis_size("age")
    pair_count = pair_target.shape[-1]
    capacity = 2 * pair_count // group_size
    target_ids = pair_target.reshape(pair_count)
    owner_ids = pair_owner.reshape(pair_count)
    source_ids = pair_source.reshape(pair_count)
    next_ages = shifted_2(positions[..., 0], "age", -1)
    next_stations = shifted_2(positions[:, :, :, 0, :], "span", -1)
    age_keep = (
        lax.axis_index("age") * age_here + jnp.arange(age_here, dtype=jnp.int32)
        < age_here * lax.axis_size("age") - 1
    ).astype(jnp.float32)
    station_keep = (
        lax.axis_index("span") * station_here + jnp.arange(station_here, dtype=jnp.int32)
        < station_here * lax.axis_size("span") - 1
    ).astype(jnp.float32)

    def build(nodes, after_age, after_station, circulation):
        trail_end = jnp.concatenate([nodes[..., 1:], after_age[..., None]], axis=-1)
        shed_end = jnp.concatenate([nodes[:, :, :, 1:, :], after_station[:, :, :, None, :]], axis=3)
        trail_gamma = circulation[0] * age_keep
        shed_gamma = circulation[1] * station_keep[:, None]
        stacked = jnp.concatenate(
            [nodes, trail_end, shed_end, trail_gamma[None], shed_gamma[None], core_radius[None]],
            axis=0,
        )
        return jnp.transpose(stacked.reshape(12, blocks_here, age_here), (1, 0, 2))

    payload, build_pullback = jax.vjp(build, positions, next_ages, next_stations, strengths)

    def to_rows(array):
        return jnp.transpose(array.reshape(array.shape[0], blocks_here, age_here), (1, 0, 2))

    def from_rows(array):
        return jnp.transpose(array, (1, 0, 2)).reshape(shape_here)

    target_blocks = to_rows(positions)
    seed_blocks = to_rows(adjoint_seed) * time_step
    owner_onehot = (owner_ids[:, None] == jnp.arange(group_size, dtype=jnp.int32)[None, :]).astype(
        jnp.int32
    )
    rank_within = jnp.sum((jnp.cumsum(owner_onehot, axis=0) - owner_onehot) * owner_onehot, axis=1)
    slot_index = owner_ids * capacity + rank_within
    request = (
        jnp.zeros((group_size * capacity,), jnp.int32)
        .at[slot_index]
        .set(source_ids)
        .reshape(group_size, capacity)
    )
    asked = lax.all_to_all(
        request, ("turb", "age"), split_axis=0, concat_axis=0, tiled=True
    ).reshape(group_size * capacity)
    pair_targets = target_blocks[target_ids]
    pair_seed = seed_blocks[target_ids]
    outgoing = (
        jnp.zeros((group_size * capacity, 6, age_here), jnp.float32)
        .at[slot_index]
        .set(jnp.concatenate([pair_targets, pair_seed], axis=1))
    )
    incoming = lax.all_to_all(
        outgoing.reshape(group_size, capacity, 6, age_here),
        ("turb", "age"),
        split_axis=0,
        concat_axis=0,
        tiled=True,
    )
    incoming = incoming.reshape(group_size * capacity, 6, age_here)
    slot_velocity, slot_grad, payload_terms = run_pairs(
        incoming[:, 0:3], payload[asked], incoming[:, 3:6]
    )
    results = jnp.concatenate([slot_velocity, slot_grad], axis=1).reshape(
        group_size, capacity, 6, age_here
    )
    answered = lax.all_to_all(
        results, ("turb", "age"), split_axis=0, concat_axis=0, tiled=True
    ).reshape(group_size * capacity, 6, age_here)[slot_index]
    pair_velocity = answered[:, 0:3]
    pair_grad = answered[:, 3:6]
    payload_grad = onehot_sum(asked, blocks_here, payload_terms)
    velocity = onehot_sum(target_ids, blocks_here, pair_velocity)
    target_grad = onehot_sum(target_ids, blocks_here, pair_grad)
    advected = positions + time_step * from_rows(velocity)
    advected = advected.at[0].add(time_step)
    grad_nodes, grad_after_age, grad_after_station, grad_strengths = build_pullback(payload_grad)
    from_prior_age = shifted_2(grad_after_age, "age", 1)
    from_prior_station = shifted_2(grad_after_station, "span", 1)
    grad_positions = adjoint_seed + grad_nodes + from_rows(target_grad)
    grad_positions = grad_positions.at[..., 0].add(from_prior_age)
    grad_positions = grad_positions.at[:, :, :, 0, :].add(from_prior_station)
    return (advected, grad_positions, grad_strengths)


def solution(mesh):
    placed = (
        P(None, "turb", None, "span", "age"),
        P(None, "turb", None, "span", "age"),
        P("turb", None, "span", "age"),
        P(None, "turb", None, "span", "age"),
        P("turb", "age", "span", None),
        P("turb", "age", "span", None),
        P("turb", "age", "span", None),
    )
    return jax.shard_map(
        local,
        mesh=mesh,
        in_specs=placed,
        out_specs=(
            P(None, "turb", None, "span", "age"),
            P(None, "turb", None, "span", "age"),
            P(None, "turb", None, "span", "age"),
        ),
        check_vma=False,
    )
```

profile of v0, /device:TPU:0, one launch (start us, length us, event | category | flops | bytes accessed | tf_op | source)
XLA Modules:
  0.0 229.6 jit_solution(2357762001795258892)
XLA Ops:
  0.6 0.7 fusion.91
  1.5 0.8 select_reduce_fusion
  3.0 1.1 scatter_custom_fusion.1
  4.2 0.7 all_to_all.13
  4.8 7.3 %all-to-all-start.1 = ((s32[8,1,32]{2,1,0:T(1,128)}), s32[8,1,32]{2,1,0:T(1,128)S(1)}, u32[]{:S(2)}, u32[]{:S(2)}) async-start(s32[8,1,32]{2,1,0:T(1,128)} %all_to_all.13), calls=%async_computation.1 | async-start | bytes 8192 | tf_op jit(solution)/shard_map/all_to_all | solution.py:162
  12.1 1.0 copy.396
  13.8 0.9 broadcast_multiply_fusion
  14.8 0.8 gather_fusion
  15.6 0.8 gather_fusion.1
  16.5 4.3 %scatter_fusion = f32[256,6,128]{2,1,0:T(8,128)S(1)} fusion(f32[256,6,128]{2,1,0:T(8,128)S(1)} %broadcast_in_dim.146, s32[128]{0:T(128)S(1)} %fusion.99, f32[128,6,128]{2,1,0:T(8,128)S(1)} %pad_maximum_fusion.2), kind=kCustom, calls=%fused_computation.4 | custom fusion | bytes 1180160 | tf_op jit(solution)/shard_map/scatter | solution.py:170
  20.9 1.0 copy.398
  21.9 6.0 %all-to-all-start = ((f32[8,32,6,128]{3,1,2,0:T(8,128)}), f32[8,32,6,128]{3,1,2,0:T(8,128)}, u32[]{:S(2)}, u32[]{:S(2)}) async-start(f32[8,32,6,128]{3,1,2,0:T(8,128)} %copy.398), calls=%async_computation | async-start | bytes 1572864 | tf_op jit(solution)/shard_map/all_to_all | solution.py:172
  28.0 1.3 collective-permute-start
  29.4 1.3 collective-permute-start.1
  31.1 3.8 %collective-permute-done = f32[3,2,3,16]{3,1,2,0:T(2,128)S(1)} collective-permute-done((f32[3,2,3,16]{3,1,2,0:T(2,128)S(1)}, f32[3,2,3,16]{3,1,2,0:T(2,128)S(1)}, u32[]{:S(2)}, u32[]{:S(2)}) %collective-permute-start) | collective-permute-done | bytes 1184 | tf_op jit(solution)/shard_map/ppermute | solution.py:19
  36.8 1.2 concatenate.69
  38.0 1.0 gather_fusion.2
  39.0 1.7 copy.409
  40.7 7.8 %all-to-all-done = f32[8,32,6,128]{3,1,2,0:T(8,128)} async-done(((f32[8,32,6,128]{3,1,2,0:T(8,128)}), f32[8,32,6,128]{3,1,2,0:T(8,128)}, u32[]{:S(2)}, u32[]{:S(2)}) %all-to-all-start) | async-done | bytes 786464 | tf_op jit(solution)/shard_map/all_to_all | solution.py:172
  48.5 1.2 copy.399
  49.8 145.9 %while.19 = (s32[]{:T(128)}, f32[16,16,3,128]{3,1,0,2:T(8,128)}, f32[16,16,3,128]{3,1,0,2:T(8,128)}, f32[16,16,12,128]{3,1,2,0:T(8,128)S(1)}, f32[16,16,3,128]{3...) while((s32[]{:T(128)}, f32[16,16,3,128]{3,1,0,2:T(8,128)}, ...), condition=%wide.region_27.28_spmd, body=%wide.region_4.27_spmd.sunk | while | flops 23116816 | bytes 65112820 | solution.py:91
  49.8 0.9 dynamic-slice_bitcast_fusion.7
  51.5 0.9 dynamic-slice_dynamic-update-slice_fusion.2
  58.9 0.9 dynamic-slice_bitcast_fusion.7
  60.6 0.9 dynamic-slice_dynamic-update-slice_fusion.2
  68.0 0.9 dynamic-slice_bitcast_fusion.7
  69.7 0.9 dynamic-slice_dynamic-update-slice_fusion.2
  76.5 0.7 bitcast_dynamic-update-slice_fusion.2
  77.2 0.9 dynamic-slice_bitcast_fusion.7
  78.9 0.9 dynamic-slice_dynamic-update-slice_fusion.2
  86.3 0.9 dynamic-slice_bitcast_fusion.7
  88.0 0.9 dynamic-slice_dynamic-update-slice_fusion.2
  95.4 0.9 dynamic-slice_bitcast_fusion.7
  97.1 0.9 dynamic-slice_dynamic-update-slice_fusion.2
  104.5 0.9 dynamic-slice_bitcast_fusion.7
  106.2 0.9 dynamic-slice_dynamic-update-slice_fusion.2
  113.7 0.9 dynamic-slice_bitcast_fusion.7
  115.3 0.9 dynamic-slice_dynamic-update-slice_fusion.2
  122.8 0.9 dynamic-slice_bitcast_fusion.7
  124.4 0.9 dynamic-slice_dynamic-update-slice_fusion.2
  131.9 0.9 dynamic-slice_bitcast_fusion.7
  133.5 0.9 dynamic-slice_dynamic-update-slice_fusion.2
  141.0 0.9 dynamic-slice_bitcast_fusion.7
  142.7 0.9 dynamic-slice_dynamic-update-slice_fusion.2
  150.1 0.9 dynamic-slice_bitcast_fusion.7
  151.8 0.9 dynamic-slice_dynamic-update-slice_fusion.2
  159.2 0.9 dynamic-slice_bitcast_fusion.7
  160.9 0.9 dynamic-slice_dynamic-update-slice_fusion.2
  168.3 0.9 dynamic-slice_bitcast_fusion.7
  170.0 0.9 dynamic-slice_dynamic-update-slice_fusion.2
  177.5 0.9 dynamic-slice_bitcast_fusion.7
  179.1 0.9 dynamic-slice_dynamic-update-slice_fusion.2
  186.6 0.9 dynamic-slice_bitcast_fusion.7
  188.2 0.9 dynamic-slice_dynamic-update-slice_fusion.2
  195.7 1.2 pad_maximum_fusion.1
  196.9 1.0 copy.413
  197.8 8.0 %all-to-all-start.2 = ((f32[8,32,6,128]{3,1,2,0:T(8,128)}), f32[8,32,6,128]{3,1,2,0:T(8,128)}, u32[]{:S(2)}, u32[]{:S(2)}) async-start(f32[8,32,6,128]{3,1,2,0:T(8,128)} %copy.413), calls=%async_computation.2 | async-start | bytes 1572864 | tf_op jit(solution)/shard_map/all_to_all | solution.py:186
  207.6 0.9 convolution_bitcast_fusion
  208.8 4.1 %collective-permute-start.2 = (f32[3,2,3,16]{3,1,2,0:T(2,128)S(1)}, f32[3,2,3,16]{3,1,2,0:T(2,128)S(1)}, u32[]{:S(2)}, u32[]{:S(2)}) collective-permute-start(f32[3,2,3,16]{3,1,2,0:T(2,128)S(1)} %bitcast.585), channel_id=1, source_target_pairs={{0,4},{4,8},{8,12},{1,5},{5,9},{9,13},{2,6},{6,10},{10,14},{3,7},{... | collective-permute-start | bytes 3464 | tf_op jit(solution)/shard_map/ppermute | solution.py:19
  213.0 1.3 collective-permute-start.3
  215.0 1.9 collective-permute-done.2
  217.1 7.8 %all-to-all-done.2 = f32[8,32,6,128]{3,1,2,0:T(8,128)} async-done(((f32[8,32,6,128]{3,1,2,0:T(8,128)}), f32[8,32,6,128]{3,1,2,0:T(8,128)}, u32[]{:S(2)}, u32[]{:S(2)}) %all-to-all-start.2) | async-done | bytes 786464 | tf_op jit(solution)/shard_map/all_to_all | solution.py:186
  224.9 1.6 copy.414
  226.6 0.8 gather_fusion.3
  (940 shorter events, 120.0 us)
Async XLA Ops:
  4.8 17.0 %all-to-all-start.1 = ((s32[8,1,32]{2,1,0:T(1,128)}), s32[8,1,32]{2,1,0:T(1,128)S(1)}, u32[]{:S(2)}, u32[]{:S(2)}) async-start(s32[8,1,32]{2,1,0:T(1,128)} %all_to_all.13), calls=%async_computation.1 | async-start | bytes 8192 | tf_op jit(solution)/shard_map/all_to_all | solution.py:162
  20.8 7.1 %copy-start = (f32[3,2,3,16,128]{4,3,2,1,0:T(8,128)S(1)}, f32[3,2,3,16,128]{4,3,2,1,0:T(8,128)}, u32[]{:S(2)}) copy-start(f32[3,2,3,16,128]{4,3,2,1,0:T(8,128)} %param.15) | copy-start | bytes 442372
  20.8 9.9 %copy-start.5 = (f32[2,2,3,16,128]{4,3,2,1,0:T(8,128)S(1)}, f32[2,2,3,16,128]{4,3,2,1,0:T(8,128)}, u32[]{:S(2)}) copy-start(f32[2,2,3,16,128]{4,3,2,1,0:T(8,128)} %param.16) | copy-start | bytes 294916
  21.9 26.6 %all-to-all-start = ((f32[8,32,6,128]{3,1,2,0:T(8,128)}), f32[8,32,6,128]{3,1,2,0:T(8,128)}, u32[]{:S(2)}, u32[]{:S(2)}) async-start(f32[8,32,6,128]{3,1,2,0:T(8,128)} %copy.398), calls=%async_computation | async-start | bytes 1572864 | tf_op jit(solution)/shard_map/all_to_all | solution.py:172
  27.9 8.9 %copy-start.6 = (f32[2,3,16,128]{3,2,1,0:T(8,128)S(1)}, f32[2,3,16,128]{3,2,1,0:T(8,128)}, u32[]{:S(2)}) copy-start(f32[2,3,16,128]{3,2,1,0:T(8,128)} %param.17) | copy-start | bytes 147460
  28.0 6.8 %collective-permute-start = (f32[3,2,3,16]{3,1,2,0:T(2,128)S(1)}, f32[3,2,3,16]{3,1,2,0:T(2,128)S(1)}, u32[]{:S(2)}, u32[]{:S(2)}) collective-permute-start(f32[3,2,3,16]{3,1,2,0:T(2,128)S(1)} %bitcast.584), channel_id=1, source_target_pairs={{4,0},{8,4},{12,8},{5,1},{9,5},{13,9},{6,2},{10,6},{14,10},{7,3},{... | collective-permute-start | bytes 3464 | tf_op jit(solution)/shard_map/ppermute | solution.py:19
  29.4 7.2 %collective-permute-start.1 = (f32[3,2,3,128]{3,1,2,0:T(2,128)S(1)}, f32[3,2,3,128]{3,1,2,0:T(2,128)S(1)}, u32[]{:S(2)}, u32[]{:S(2)}) collective-permute-start(f32[3,2,3,128]{3,1,2,0:T(2,128)S(1)} %bitcast.588), channel_id=1, source_target_pairs={{1,0},{2,1},{3,2},{5,4},{6,5},{7,6},{9,8},{10,9},{11,10},{13,12},{... | collective-permute-start | bytes 27656 | tf_op jit(solution)/shard_map/ppermute | solution.py:19
  40.7 9.1 %copy-start.1 = (f32[16,16,12,128]{3,1,2,0:T(8,128)S(1)}, f32[16,16,12,128]{3,1,2,0:T(8,128)}, u32[]{:S(2)}) copy-start(f32[16,16,12,128]{3,1,2,0:T(8,128)} %custom-call.11) | copy-start | bytes 4718596
  197.8 27.1 %all-to-all-start.2 = ((f32[8,32,6,128]{3,1,2,0:T(8,128)}), f32[8,32,6,128]{3,1,2,0:T(8,128)}, u32[]{:S(2)}, u32[]{:S(2)}) async-start(f32[8,32,6,128]{3,1,2,0:T(8,128)} %copy.413), calls=%async_computation.2 | async-start | bytes 1572864 | tf_op jit(solution)/shard_map/all_to_all | solution.py:186
  208.8 8.1 %collective-permute-start.2 = (f32[3,2,3,16]{3,1,2,0:T(2,128)S(1)}, f32[3,2,3,16]{3,1,2,0:T(2,128)S(1)}, u32[]{:S(2)}, u32[]{:S(2)}) collective-permute-start(f32[3,2,3,16]{3,1,2,0:T(2,128)S(1)} %bitcast.585), channel_id=1, source_target_pairs={{0,4},{4,8},{8,12},{1,5},{5,9},{9,13},{2,6},{6,10},{10,14},{3,7},{... | collective-permute-start | bytes 3464 | tf_op jit(solution)/shard_map/ppermute | solution.py:19
  213.0 15.2 %collective-permute-start.3 = (f32[3,2,3,128]{3,1,2,0:T(2,128)S(1)}, f32[3,2,3,128]{3,1,2,0:T(2,128)S(1)}, u32[]{:S(2)}, u32[]{:S(2)}) collective-permute-start(f32[3,2,3,128]{3,1,2,0:T(2,128)S(1)} %bitcast.590), channel_id=1, source_target_pairs={{0,1},{1,2},{2,3},{4,5},{5,6},{6,7},{8,9},{9,10},{10,11},{12,13},{... | collective-permute-start | bytes 27656 | tf_op jit(solution)/shard_map/ppermute | solution.py:19
  226.5 1.0 copy-start.7
  226.6 1.3 copy-start.3
  228.3 0.7 copy-start.2
  229.0 0.7 copy-start.4
where the time goes:
time: 231 us; the launch traced here: 230 us
  other arithmetic  92.8 us (40%)
  local copies, waits for them, and re-layouts  77.9 us (34%)
  starting transfers between devices  29.2 us (13%)
  waiting for transfers between devices  21.4 us (9%)
  loops' own time  5.59 us (2%)
    while x272, local copies, waits for them, and re-layouts  34.7 us
    squeeze x32, local copies, waits for them, and re-layouts, run_pairs(): velocity, grad_targets, grad_payload = lax.map(one_batch, shaped)  14.6 us
    dynamic_update_slice x32, other arithmetic, run_pairs(): velocity, grad_targets, grad_payload = lax.map(one_batch, shaped)  14.2 us
    add_any x16, other arithmetic, windows(): padded[:, :, REACH + offset:REACH + offset + age_count]  9.18 us
    reduce_sum x32, other arithmetic, induced(): length_sq = jnp.sum(along * along, axis=-2) + core_sq  8.08 us
    all_to_all x1, starting transfers between devices, local(): lax.all_to_all(results, ('turb', 'age'), split_axis=0, concat_axis=0, til...  7.99 us
    ppermute x4, starting transfers between devices, shifted_2(): lax.ppermute(value, axis, [(source, source + steps) for source in range(l...  7.98 us
    all_to_all x1, waiting for transfers between devices, local(): lax.all_to_all(outgoing.reshape(group_size, capacity, 6, age_here), ('tur...  7.84 us
  transfers between devices with their start and end apart: 7, of which 4 were waited for; matrix products, arithmetic and copies ran while one was open for 10% of the time, Pallas kernels for 0%

commit v1 on v0

--- a/solution.py
+++ b/solution.py
@@ -1,8 +1,11 @@
+import functools
 import math
 
 import jax
 import jax.numpy as jnp
 from jax import lax
+from jax.experimental import pallas as pl
+from jax.experimental.pallas import tpu as pltpu
 from jax.sharding import PartitionSpec as P
 
 REACH = 8
@@ -105,7 +108,7 @@
     return summed.reshape((rows,) + values.shape[1:])
 
 
-def local(positions, strengths, core_radius, adjoint_seed, pair_target, pair_owner, pair_source):
+def local_sparse(positions, strengths, core_radius, adjoint_seed, pair_target, pair_owner, pair_source):
     shape_here = positions.shape
     station_here = shape_here[3]
     age_here = shape_here[4]
@@ -202,6 +205,290 @@
     return (advected, grad_positions, grad_strengths)
 
 
+TILE = 8
+SRC_ROWS = 16
+TGT_ROWS = 8
+
+
+def cross(a, b):
+    return (
+        a[1] * b[2] - a[2] * b[1],
+        a[2] * b[0] - a[0] * b[2],
+        a[0] * b[1] - a[1] * b[0],
+    )
+
+
+def dot(a, b):
+    return a[0] * b[0] + a[1] * b[1] + a[2] * b[2]
+
+
+def segment(r0, r1, r2, inv1, cube1, gamma, core_sq, quad, quart, inside, w):
+    c = cross(r0, r1)
+    c_sq = dot(c, c)
+    a = dot(r0, r1)
+    b = dot(r0, r2)
+    inv2 = lax.rsqrt(dot(r2, r2) + core_sq)
+    proj = a * inv1 - b * inv2
+    inv_d = lax.rsqrt(c_sq * c_sq + quart)
+    inv_d = jnp.where(inside, inv_d, 0.0)
+    q = dot(w, c)
+    m = gamma * inv_d
+    k = m * proj
+    gp = m * q
+    fd = (k * q) * (inv_d * inv_d)
+    grad_gamma = proj * (q * inv_d)
+    h = 2.0 * fd * c_sq
+    gn2 = gp * b * (inv2 * inv2 * inv2)
+    alpha = gp * (inv1 - inv2) - gn2
+    beta = gn2 - gp * a * cube1
+    delta = 2.0 * (gp * inv2 - fd * quad) + gn2
+    gc = tuple(k * w[i] - h * c[i] for i in range(3))
+    left = cross(gc, r0)
+    right = cross(r1, gc)
+    grad_r1 = tuple(left[i] + alpha * r0[i] + beta * r1[i] for i in range(3))
+    grad_r0 = tuple(right[i] + alpha * r1[i] + delta * r0[i] for i in range(3))
+    velocity = tuple(k * c[i] for i in range(3))
+    return velocity, grad_r1, grad_r0, grad_gamma
+
+
+def pair_tile(rows, ages):
+    lane = lax.broadcasted_iota(jnp.int32, (TILE, ages), 1)
+    begin = rows[0:3]
+    core = rows[5]
+    core_sq = core * core
+    trail = [
+        jnp.where(
+            lane == ages - 1,
+            pltpu.roll(rows[6 + i], ages - 1, 1),
+            pltpu.roll(begin[i], ages - 1, 1),
+        )
+        for i in range(3)
+    ]
+    alongs = [[trail[i] - begin[i] for i in range(3)], [rows[9 + i] - begin[i] for i in range(3)]]
+    gammas = [rows[3] * (1.0 / four_pi), rows[4] * (1.0 / four_pi)]
+    core_quad = core_sq * core_sq
+    lengths = [dot(r0, r0) + core_sq for r0 in alongs]
+    quads = [core_quad * length for length in lengths]
+    quarts = [quad * length for quad, length in zip(quads, lengths)]
+    zero = jnp.zeros((TILE, ages), jnp.float32)
+    sum_r1 = [zero] * 3
+    sum_r0 = [[zero] * 3, [zero] * 3]
+    sum_gamma = [zero, zero]
+    out = [zero] * 6
+    for offset in range(-REACH, REACH):
+        shift = offset % ages
+        moved = [pltpu.roll(x, shift, 1) if shift else x for x in rows[12:18]]
+        target, w = moved[0:3], moved[3:6]
+        if offset >= 0:
+            inside = lane >= offset
+        else:
+            inside = lane < ages + offset
+        r1 = [target[i] - begin[i] for i in range(3)]
+        inv1 = lax.rsqrt(dot(r1, r1) + core_sq)
+        cube1 = inv1 * inv1 * inv1
+        vel = [None] * 3
+        g1 = [None] * 3
+        for kind in range(2):
+            r0 = alongs[kind]
+            r2 = [r1[i] - r0[i] for i in range(3)]
+            v, d1, d0, dg = segment(
+                r0, r1, r2, inv1, cube1, gammas[kind], core_sq,
+                quads[kind], quarts[kind], inside, w,
+            )
+            vel = [v[i] if kind == 0 else vel[i] + v[i] for i in range(3)]
+            g1 = [d1[i] if kind == 0 else g1[i] + d1[i] for i in range(3)]
+            sum_r0[kind] = [sum_r0[kind][i] + d0[i] for i in range(3)]
+            sum_gamma[kind] = sum_gamma[kind] + dg
+        sum_r1 = [sum_r1[i] + g1[i] for i in range(3)]
+        back = (-offset) % ages
+        both = vel + g1
+        out = [out[i] + (pltpu.roll(both[i], back, 1) if back else both[i]) for i in range(6)]
+    grad_begin = [-(sum_r1[i] + sum_r0[0][i] + sum_r0[1][i]) for i in range(3)]
+    grad_source = grad_begin + sum_r0[0] + sum_r0[1] + [g * (1.0 / four_pi) for g in sum_gamma]
+    return grad_source, out
+
+
+def pairs_kernel(
+    group, blocks, stations, per_owner, grad_rows, index_ref, table_ref, seed_ref,
+    grad_ref, out_ref, rows_buf, src_buf, tgt_buf, acc, tgt_acc,
+):
+    pairs = index_ref.shape[1]
+    ages = table_ref.shape[-1]
+    halo = blocks // stations
+    acc[...] = jnp.zeros_like(acc)
+    tgt_acc[...] = jnp.zeros_like(tgt_acc)
+
+    def tile(t, _):
+        for j in range(TILE):
+            p = t * TILE + j
+            src = index_ref[0, p]
+            nxt = index_ref[1, p]
+            shed = index_ref[2, p]
+            shed_step = index_ref[3, p]
+            own = index_ref[4, p]
+            tgt = index_ref[5, p]
+            for r in range(6):
+                rows_buf[pl.ds(r * TILE + j, 1), :] = table_ref[pl.ds(src + r * blocks, 1), :]
+            for r in range(3):
+                rows_buf[pl.ds((6 + r) * TILE + j, 1), :] = table_ref[pl.ds(nxt + r * blocks, 1), :]
+                rows_buf[pl.ds((9 + r) * TILE + j, 1), :] = table_ref[pl.ds(shed + r * shed_step, 1), :]
+                rows_buf[pl.ds((12 + r) * TILE + j, 1), :] = table_ref[pl.ds(own + r * blocks, 1), :]
+                rows_buf[pl.ds((15 + r) * TILE + j, 1), :] = seed_ref[pl.ds(tgt + r * blocks, 1), :]
+        rows = [rows_buf[pl.ds(r * TILE, TILE), :] for r in range(18)]
+        grad_source, out = pair_tile(rows, ages)
+        for r in range(11):
+            src_buf[pl.ds(t * (TILE * SRC_ROWS) + r, TILE, stride=SRC_ROWS), :] = grad_source[r]
+        for r in range(6):
+            tgt_buf[pl.ds(t * (TILE * TGT_ROWS) + r, TILE, stride=TGT_ROWS), :] = out[r]
+        return 0
+
+    lax.fori_loop(0, pairs // TILE, tile, 0)
+
+    def scatter(p, _):
+        at = pl.ds(pl.multiple_of(index_ref[6, p], SRC_ROWS), SRC_ROWS)
+        acc[at, :] += src_buf[pl.ds(pl.multiple_of(p * SRC_ROWS, SRC_ROWS), SRC_ROWS), :]
+        at = pl.ds(pl.multiple_of(index_ref[5, p] * TGT_ROWS, TGT_ROWS), TGT_ROWS)
+        tgt_acc[at, :] += tgt_buf[pl.ds(pl.multiple_of(p * TGT_ROWS, TGT_ROWS), TGT_ROWS), :]
+        return 0
+
+    lax.fori_loop(0, pairs, scatter, 0, unroll=8)
+
+    for c in range(6):
+        for q in range(0, blocks, 8):
+            out_ref[pl.ds(c * blocks + q, 8), :] = tgt_acc[pl.ds(q * TGT_ROWS + c, 8, stride=TGT_ROWS), :]
+
+    lane = lax.broadcasted_iota(jnp.int32, (TILE, ages), 1)
+    sub = lax.broadcasted_iota(jnp.int32, (TILE, ages), 0)
+
+    def fold(o, _):
+        prev = lax.rem(o + group - 1, group)
+
+        def rows_of(owner, q, r):
+            return acc[pl.ds((owner * blocks + q + 1) * SRC_ROWS + r, 8, stride=SRC_ROWS), :]
+
+        base = o * grad_rows
+        for q in range(0, blocks, 8):
+            for c in range(3):
+                trail = jnp.where(lane == ages - 1, rows_of(prev, q, 3 + c), rows_of(o, q, 3 + c))
+                shed = rows_of(o, q - 1, 6 + c)
+                if q % stations == 0:
+                    shed = jnp.where(sub == 0, 0.0, shed)
+                grad_ref[pl.ds(base + c * blocks + q, 8), :] = (
+                    rows_of(o, q, c) + pltpu.roll(trail, 1, 1) + shed
+                )
+            for c in range(2):
+                grad_ref[pl.ds(base + (3 + c) * blocks + q, 8), :] = rows_of(o, q, 9 + c)
+        for c in range(3):
+            for h in range(halo):
+                row = (o * blocks + h * stations + stations) * SRC_ROWS + 6 + c
+                grad_ref[pl.ds(base + 5 * blocks + c * halo + h, 1), :] = acc[pl.ds(row, 1), :]
+        grad_ref[pl.ds(base + 5 * blocks + 3 * halo, grad_rows - 5 * blocks - 3 * halo), :] = (
+            jnp.zeros((grad_rows - 5 * blocks - 3 * halo, ages), jnp.float32)
+        )
+        return 0
+
+    lax.fori_loop(0, group, fold, 0)
+
+
+def local_dense(positions, strengths, core_radius, adjoint_seed, pair_target, pair_owner, pair_source):
+    shape_here = positions.shape
+    stations = shape_here[3]
+    ages = shape_here[4]
+    blocks = shape_here[1] * shape_here[2] * stations
+    halo = blocks // stations
+    group = lax.axis_size("turb") * lax.axis_size("age")
+    pairs = pair_target.shape[-1]
+    per_owner = -(-(6 * blocks + 3 * halo) // 8) * 8
+    grad_rows = -(-(5 * blocks + 3 * halo) // 8) * 8
+    target_ids = pair_target.reshape(pairs)
+    owner_ids = pair_owner.reshape(pairs)
+    source_ids = pair_source.reshape(pairs)
+    age_keep = (
+        lax.axis_index("age") * ages + jnp.arange(ages, dtype=jnp.int32)
+        < ages * lax.axis_size("age") - 1
+    ).astype(jnp.float32)
+    station_keep = (
+        lax.axis_index("span") * stations + jnp.arange(stations, dtype=jnp.int32)
+        < stations * lax.axis_size("span") - 1
+    ).astype(jnp.float32)[:, None]
+    me = lax.axis_index("turb") * lax.axis_size("age") + lax.axis_index("age")
+    next_stations = shifted_2(positions[:, :, :, 0, :], "span", -1)
+    payload = jnp.concatenate(
+        [
+            positions.reshape(3 * blocks, ages),
+            (strengths[0] * age_keep).reshape(blocks, ages),
+            (strengths[1] * station_keep).reshape(blocks, ages),
+            core_radius.reshape(blocks, ages),
+            next_stations.reshape(3 * halo, ages),
+            jnp.zeros((per_owner - 6 * blocks - 3 * halo, ages), jnp.float32),
+        ]
+    )
+    table = lax.all_gather(payload, ("turb", "age"), axis=0, tiled=True)
+    station = source_ids % stations
+    inner = station < stations - 1
+    base = owner_ids * per_owner
+    index = jnp.stack(
+        [
+            base + source_ids,
+            (owner_ids + 1) % group * per_owner + source_ids,
+            base + jnp.where(inner, source_ids + 1, 6 * blocks + source_ids // stations),
+            jnp.where(inner, blocks, halo),
+            me * per_owner + target_ids,
+            target_ids,
+            (owner_ids * blocks + source_ids + 1) * SRC_ROWS,
+            target_ids,
+        ]
+    )
+    seed_rows = adjoint_seed.reshape(3 * blocks, ages) * time_step
+    vmem = pl.BlockSpec(memory_space=pltpu.VMEM)
+    grads, sums = pl.pallas_call(
+        functools.partial(pairs_kernel, group, blocks, stations, per_owner, grad_rows),
+        out_shape=(
+            jax.ShapeDtypeStruct((group * grad_rows, ages), jnp.float32),
+            jax.ShapeDtypeStruct((6 * blocks, ages), jnp.float32),
+        ),
+        in_specs=[pl.BlockSpec(memory_space=pltpu.SMEM), vmem, vmem],
+        out_specs=(vmem, vmem),
+        scratch_shapes=[
+            pltpu.VMEM((18 * TILE, ages), jnp.float32),
+            pltpu.VMEM((pairs * SRC_ROWS, ages), jnp.float32),
+            pltpu.VMEM((pairs * TGT_ROWS, ages), jnp.float32),
+            pltpu.VMEM(((group * blocks + 1) * SRC_ROWS, ages), jnp.float32),
+            pltpu.VMEM((blocks * TGT_ROWS, ages), jnp.float32),
+        ],
+        compiler_params=pltpu.CompilerParams(vmem_limit_bytes=40 * 1024 * 1024),
+    )(index, table, seed_rows)
+    mine = lax.psum_scatter(grads, ("turb", "age"), scatter_dimension=0, tiled=True)
+    advected = positions + time_step * sums[: 3 * blocks].reshape(shape_here)
+    advected = advected.at[0].add(time_step)
+    grad_positions = (
+        adjoint_seed
+        + sums[3 * blocks :].reshape(shape_here)
+        + mine[: 3 * blocks].reshape(shape_here)
+    )
+    from_prior = shifted_2(
+        mine[5 * blocks : 5 * blocks + 3 * halo].reshape(shape_here[:3] + (ages,)), "span", 1
+    )
+    grad_positions = grad_positions.at[:, :, :, 0, :].add(from_prior)
+    grad_strengths = mine[3 * blocks : 5 * blocks].reshape(strengths.shape)
+    grad_strengths = grad_strengths * jnp.stack(
+        [
+            jnp.broadcast_to(age_keep[None], (stations, ages)),
+            jnp.broadcast_to(station_keep, (stations, ages)),
+        ]
+    )[:, None, None]
+    return (advected, grad_positions, grad_strengths)
+
+
+def local(positions, strengths, core_radius, adjoint_seed, pair_target, pair_owner, pair_source):
+    blocks = positions.shape[1] * positions.shape[2] * positions.shape[3]
+    group = lax.axis_size("turb") * lax.axis_size("age")
+    chosen = local_dense if group * blocks <= 8 * pair_target.shape[-1] else local_sparse
+    return chosen(
+        positions, strengths, core_radius, adjoint_seed, pair_target, pair_owner, pair_source
+    )
+
+
 def solution(mesh):
     placed = (
         P(None, "turb", None, "span", "age"),

time: 231 us -> 207 us (0.90)
  waiting for transfers between devices: 21.4 us -> 152 us
  other arithmetic: 92.8 us -> 3.1 us
  local copies, waits for them, and re-layouts: 77.9 us -> 14.3 us
  starting transfers between devices: 29.2 us -> 2.89 us
  Pallas kernels: 0 us -> 17.6 us
  between operations: 1.17 us -> 14.9 us
  loops' own time: 5.59 us -> 0 us
    unnamed x0 -> x3, waiting for transfers between devices: none -> 97.9 us
    all_gather x0 -> x1, waiting for transfers between devices: none -> 53.3 us  [local_dense(): table = lax.all_gather(payload, ('turb', 'age'), axis=0, tiled=True)]
    while x274 -> x0, local copies, waits for them, and re-layouts: 36.9 us -> none
    reduce_sum x145 -> x0, other arithmetic: 28.9 us -> none  [the longest x32 8.08 us: induced(): length_sq = jnp.sum(along * along, axis=-2) + core_sq]
    all_to_all x3 -> x0, starting transfers between devices: 21.2 us -> none  [the longest x1 7.99 us: local(): lax.all_to_all(results, ('turb', 'age'), split_axis=0, concat_axis=0, til...]
    add_any x65 -> x0, other arithmetic: 18.9 us -> none  [the longest x16 9.18 us: windows(): padded[:, :, REACH + offset:REACH + offset + age_count]]
    pallas_call x0 -> x1, Pallas kernels: none -> 17.6 us  [local_dense(): pl.pallas_call(functools.partial(pairs_kernel, group, blocks, stations, p...]
    all_to_all x3 -> x0, waiting for transfers between devices: 15.7 us -> none  [the longest x1 7.84 us: local(): lax.all_to_all(outgoing.reshape(group_size, capacity, 6, age_here), ('tur...]
  transfers between devices with their start and end apart: 7 -> 4, of which waited for: 4 -> 3; matrix products, arithmetic and copies ran while one was open for 10% -> 4% of each run, Pallas kernels for 0% -> 0%
where the time goes in v1:
time: 207 us; the launch traced here: 205 us
  waiting for transfers between devices  152 us (73%)
  Pallas kernels  17.6 us (9%)
  between operations  14.9 us (7%)
  local copies, waits for them, and re-layouts  14.3 us (7%)
  other arithmetic  3.1 us (1%)
  starting transfers between devices  2.89 us (1%)
    unnamed x3, waiting for transfers between devices  97.9 us
    all_gather x1, waiting for transfers between devices, local_dense(): table = lax.all_gather(payload, ('turb', 'age'), axis=0, tiled=True)  53.3 us
    pallas_call x1, Pallas kernels, local_dense(): pl.pallas_call(functools.partial(pairs_kernel, group, blocks, stations, p...  17.6 us
    concatenate x1, local copies, waits for them, and re-layouts, local_dense(): jnp.concatenate([positions.reshape(3 * blocks, ages), (strengths[0] * age...  6.07 us
  transfers between devices with their start and end apart: 4, of which 3 were waited for; matrix products, arithmetic and copies ran while one was open for 4% of the time, Pallas kernels for 0%

profile of v1, /device:TPU:0, one launch (start us, length us, event | category | flops | bytes accessed | tf_op | source)
XLA Modules:
  0.0 204.8 jit_solution(18039972635289483983)
XLA Ops:
  7.2 0.0 all-gather.2.cloned.1.call-start
  7.2 0.9 slice.90
  8.1 1.3 collective-permute-start
  9.5 0.1 mul.124
  9.5 0.8 fusion.8
  10.4 0.1 bitcast_multiply_fusion
  10.5 0.7 collective-permute-done
  11.2 6.1 %concatenate.7 = f32[600,128]{1,0:T(8,128)} concatenate(f32[288,128]{1,0:T(8,128)} %bitcast.53, f32[96,128]{1,0:T(8,128)S(1)} %get-tuple-element.47, f32[96,128]{1,0:T(8,128)S(1)} %get-tuple-element.46, f32[96,128]{1,0:T(8,128)} %bitcast.58, f32[18,128]{1,0:T(8,128)S(1)} %reshape.391, f32[6,128]{1,0:T(8,128)S(1)} %broadcast_in_dim.21), dimensions={0} | concatenate | bytes 614400 | tf_op jit(solution)/shard_map/concatenate | solution.py:416
  17.3 0.0 all-gather.2.cloned.1.call-update
  17.3 0.0 all-reduce.3.cloned.1.call-start
  17.4 0.7 broadcast_add_fusion
  18.0 0.7 fusion.6
  18.7 0.8 stack.4.index_ref
  19.5 0.9 broadcast_multiply_fusion
  20.4 53.3 %all-gather.2.cloned.1.call-done.table_ref = f32[4800,128]{1,0:T(8,128)} async-done(((f32[600,128]{1,0:T(8,128)}), f32[4800,128]{1,0:T(8,128)}) %all-gather.2.cloned.1.call-update) | async-done | bytes 2457616 | tf_op jit(solution)/shard_map/all_gather | solution.py:426
  73.6 0.0 copy-start
  73.6 1.7 copy-done
  75.3 0.0 copy-start.5
  75.3 0.0 copy-start.1
  75.3 17.6 %shard_map.94 = (f32[4032,128]{1,0:T(8,128)}, f32[576,128]{1,0:T(8,128)S(1)}) custom-call(s32[8,128]{1,0:T(8,128)S(1)} %stack.4.index_ref, f32[4800,128]{1,0:T(8,128)S(1)} %copy-done, f32[288,128]{1,0:T(8,128)S(1)} %bitcast.52), custom_call_target="tpu_custom_call" | custom-call | tf_op jit(solution)/shard_map/pallas_call | solution.py:444
  93.0 0.0 copy-start.2
  93.0 0.0 all-reduce.3.cloned.1.call-update
  93.0 0.0 copy-done.5
  93.0 0.6 dynamic-slice.15
  94.3 0.1 stack_broadcast_in_dim.5
  94.4 0.0 copy-done.1
  94.4 0.0 copy-start.3
  94.4 97.9 %all-reduce.3.cloned.1.call-done = f32[4032,128]{1,0:T(8,128)} async-done(((f32[4032,128]{1,0:T(8,128)}), f32[4032,128]{1,0:T(8,128)}) %all-reduce.3.cloned.1.call-update) | async-done | bytes 2064400
  192.4 0.7 constant_dynamic-slice_fusion
  193.1 1.5 collective-permute-start.1
  194.6 0.9 constant_dynamic-slice_fusion.1
  195.6 0.0 copy-done.2
  195.6 0.9 constant_dynamic-slice_fusion.2
  196.5 0.7 broadcast_multiply_fusion.1
  197.2 0.0 collective-permute-done.1
  197.2 0.1 scatter-add.9
  197.3 0.0 copy-done.3
  197.3 0.0 copy-start.4
  197.3 0.7 copy-done.4
  (15 shorter events, 0.1 us)
Async XLA Ops:
  7.2 66.5 %all-gather.2.cloned.1.call-start = ((), (), s32[]{:S(2)}) async-start(), calls=%async_computation | async-start | bytes 2764800 | tf_op jit(solution)/shard_map/all_gather | solution.py:426
  8.1 3.1 %collective-permute-start = (f32[3,2,3,128]{3,1,2,0:T(2,128)S(1)}, f32[3,2,3,128]{3,1,2,0:T(2,128)S(1)}, u32[]{:S(2)}, u32[]{:S(2)}) collective-permute-start(f32[3,2,3,128]{3,1,2,0:T(2,128)S(1)} %bitcast.60), channel_id=1, source_target_pairs={{1,0},{2,1},{3,2},{5,4},{6,5},{7,6},{9,8},{10,9},{11,10},{13,12},{... | collective-permute-start | bytes 27656 | tf_op jit(solution)/shard_map/ppermute | solution.py:22
  17.3 175.1 %all-reduce.3.cloned.1.call-start = ((), (), s32[]{:S(2)}) async-start(), calls=%async_computation.1 | async-start | bytes 4128768
  73.6 1.7 copy-start
  75.3 17.7 %copy-start.5 = (u32[32]{0:T(128)S(1)}, u32[32]{0:T(128)}, u32[]{:S(2)}) copy-start(u32[32]{0:T(128)} %constant.134) | copy-start | bytes 388
  75.3 19.0 %copy-start.1 = (f32[3,2,3,16,128]{4,3,2,1,0:T(8,128)S(1)}, f32[3,2,3,16,128]{4,3,2,1,0:T(8,128)}, u32[]{:S(2)}) copy-start(f32[3,2,3,16,128]{4,3,2,1,0:T(8,128)} %param.11) | copy-start | bytes 442372
  93.0 102.6 %copy-start.2 = (f32[3,2,3,16,128]{4,3,2,1,0:T(8,128)S(1)}, f32[3,2,3,16,128]{4,3,2,1,0:T(8,128)}, u32[]{:S(2)}) copy-start(f32[3,2,3,16,128]{4,3,2,1,0:T(8,128)} %param.14) | copy-start | bytes 442372
  94.4 102.8 %copy-start.3 = (f32[3,2,3,16,128]{4,3,2,1,0:T(8,128)}, f32[3,2,3,16,128]{4,3,2,1,0:T(8,128)S(1)}, u32[]{:S(2)}) copy-start(f32[3,2,3,16,128]{4,3,2,1,0:T(8,128)S(1)} %fusion) | copy-start | bytes 442372
  193.1 4.1 %collective-permute-start.1 = (f32[3,2,3,128]{3,2,1,0:T(4,128)S(1)}, f32[3,2,3,128]{3,2,1,0:T(4,128)S(1)}, u32[]{:S(2)}, u32[]{:S(2)}) collective-permute-start(f32[3,2,3,128]{3,2,1,0:T(4,128)S(1)} %reshape.394), channel_id=1, source_target_pairs={{0,1},{1,2},{2,3},{4,5},{5,6},{6,7},{8,9},{9,10},{10,11},{12,13},{... | collective-permute-start | bytes 27656 | tf_op jit(solution)/shard_map/ppermute | solution.py:22
  197.3 0.7 copy-start.4
Sparse Core Ops, SparseCore 0:
  17.4 56.1 all-gather.1
  93.1 99.1 all-reduce.2

commit v2 on v1

--- a/solution.py
+++ b/solution.py
@@ -333,7 +333,7 @@
                 rows_buf[pl.ds((6 + r) * TILE + j, 1), :] = table_ref[pl.ds(nxt + r * blocks, 1), :]
                 rows_buf[pl.ds((9 + r) * TILE + j, 1), :] = table_ref[pl.ds(shed + r * shed_step, 1), :]
                 rows_buf[pl.ds((12 + r) * TILE + j, 1), :] = table_ref[pl.ds(own + r * blocks, 1), :]
-                rows_buf[pl.ds((15 + r) * TILE + j, 1), :] = seed_ref[pl.ds(tgt + r * blocks, 1), :]
+                rows_buf[pl.ds((15 + r) * TILE + j, 1), :] = seed_ref[pl.ds(tgt + r * blocks, 1), :] * time_step
         rows = [rows_buf[pl.ds(r * TILE, TILE), :] for r in range(18)]
         grad_source, out = pair_tile(rows, ages)
         for r in range(11):
@@ -390,40 +390,355 @@
     lax.fori_loop(0, group, fold, 0)
 
 
+MESH = pl.DeviceIdType.MESH
+
+
+def place():
+    here = (lax.axis_index("turb"), lax.axis_index("age"), lax.axis_index("span"))
+    spans = lax.axis_size("span")
+    turb, age, span = here
+    return (
+        here,
+        (1 - turb, age, span),
+        (turb, age - 1, span),
+        (turb, age + 1, span),
+        (turb, age, lax.rem(span + spans - 1, spans)),
+        (turb, age, lax.rem(span + 1, spans)),
+    )
+
+
+def greet(ages_count):
+    here, other, below, above, prior, following = place()
+    barrier = pltpu.get_barrier_semaphore()
+    for device in (other, prior, following):
+        pl.semaphore_signal(barrier, inc=1, device_id=device, device_id_type=MESH)
+
+    @pl.when(here[1] > 0)
+    def _():
+        pl.semaphore_signal(barrier, inc=1, device_id=below, device_id_type=MESH)
+
+    @pl.when(here[1] < ages_count - 1)
+    def _():
+        pl.semaphore_signal(barrier, inc=1, device_id=above, device_id_type=MESH)
+
+    inner = (here[1] > 0).astype(jnp.int32) + (here[1] < ages_count - 1).astype(jnp.int32)
+    pl.semaphore_wait(barrier, 3 + inner)
+
+
+def keeps(stations, ages, shape):
+    lane = lax.broadcasted_iota(jnp.int32, shape, 1)
+    row = lax.broadcasted_iota(jnp.int32, shape, 0)
+    last_age = lax.axis_index("age") == lax.axis_size("age") - 1
+    last_station = lax.axis_index("span") == lax.axis_size("span") - 1
+    trail = jnp.where(jnp.logical_and(last_age, lane == ages - 1), 0.0, 1.0)
+    shed = jnp.where(jnp.logical_and(last_station, row % stations == stations - 1), 0.0, 1.0)
+    return trail, shed
+
+
+def gather_kernel(
+    blocks, stations, per_owner, positions_ref, strengths_ref, core_ref, table_ref,
+    halo_buf, halo_sems, send_sems, recv_sems,
+):
+    ages = table_ref.shape[-1]
+    count = lax.axis_size("age")
+    halo = blocks // stations
+    here, other, below, above, prior, following = place()
+    turb, age, span = here
+    split = 5 * blocks
+    me = turb * count + age
+    mate = (1 - turb) * count + age
+    extra = per_owner - 6 * blocks
+    parts = ((0, split), (split, per_owner - split))
+
+    def rows(owner, part):
+        return pl.ds(pl.multiple_of(owner * per_owner + parts[part][0], 8), parts[part][1])
+
+    def copy(owner, part, way):
+        at = rows(owner, part)
+        return pltpu.make_async_remote_copy(
+            src_ref=table_ref.at[at],
+            dst_ref=table_ref.at[at],
+            send_sem=send_sems.at[way, part, owner],
+            recv_sem=recv_sems.at[part, owner],
+            device_id=(other, below, above)[way],
+            device_id_type=MESH,
+        )
+
+    def arrive(owner, part):
+        copy(owner, part, 0).wait_recv()
+
+    base = me * per_owner
+    halo_buf[...] = jnp.zeros_like(halo_buf)
+    for k in range(3 * halo):
+        halo_buf[pl.ds(k, 1), :] = positions_ref[pl.ds(k * stations, 1), :]
+    table_ref[pl.ds(pl.multiple_of(base, 8), 3 * blocks), :] = positions_ref[...]
+    trail, shed = keeps(stations, ages, (blocks, ages))
+    table_ref[pl.ds(pl.multiple_of(base + 3 * blocks, 8), blocks), :] = (
+        strengths_ref[pl.ds(0, blocks), :] * trail
+    )
+    table_ref[pl.ds(pl.multiple_of(base + 4 * blocks, 8), blocks), :] = (
+        strengths_ref[pl.ds(blocks, blocks), :] * shed
+    )
+    table_ref[pl.ds(pl.multiple_of(base + 5 * blocks, 8), blocks), :] = core_ref[...]
+    greet(count)
+    halo_copy = pltpu.make_async_remote_copy(
+        src_ref=halo_buf,
+        dst_ref=table_ref.at[pl.ds(pl.multiple_of(base + 6 * blocks, 8), extra)],
+        send_sem=halo_sems.at[0],
+        recv_sem=halo_sems.at[1],
+        device_id=prior,
+        device_id_type=MESH,
+    )
+    halo_copy.start()
+
+    has_below = age > 0
+    has_above = age < count - 1
+
+    @pl.when(has_below)
+    def _():
+        copy(me, 0, 1).start()
+
+    @pl.when(has_above)
+    def _():
+        copy(me, 0, 2).start()
+
+    copy(me, 0, 0).start()
+    halo_copy.wait_recv()
+    copy(me, 1, 0).start()
+
+    @pl.when(has_below)
+    def _():
+        copy(me, 1, 1).start()
+
+    @pl.when(has_above)
+    def _():
+        copy(me, 1, 2).start()
+
+    arrive(mate, 1)
+
+    @pl.when(has_below)
+    def _():
+        copy(mate, 1, 1).start()
+
+    @pl.when(has_above)
+    def _():
+        copy(mate, 1, 2).start()
+
+    for step in range(1, count):
+        for way, sign in ((2, -1), (1, 1)):
+            source = age + sign * step
+            exists = source >= 0 if sign < 0 else source < count
+            onward = has_above if way == 2 else has_below
+
+            @pl.when(exists)
+            def _(source=source, way=way, onward=onward):
+                owner = turb * count + source
+                arrive(owner, 0)
+
+                @pl.when(onward)
+                def _():
+                    copy(owner, 0, way).start()
+
+                copy(owner, 0, 0).start()
+
+        for way, sign in ((2, -1), (1, 1)):
+            source = age + sign * step
+            exists = source >= 0 if sign < 0 else source < count
+            onward = has_above if way == 2 else has_below
+
+            @pl.when(exists)
+            def _(source=source, way=way, onward=onward):
+                for column in (turb, 1 - turb):
+                    owner = column * count + source
+                    arrive(owner, 1)
+
+                    @pl.when(onward)
+                    def _(owner=owner):
+                        copy(owner, 1, way).start()
+
+    for source in range(count):
+        arrive((1 - turb) * count + source, 0)
+    halo_copy.wait_send()
+    copy(me, 1, 0).wait_send()
+    for source in range(count):
+        owner = turb * count + source
+        copy(owner, 0, 0).wait_send()
+
+        @pl.when(jnp.logical_and(source >= age, has_below))
+        def _(source=source, owner=owner):
+            copy(owner, 0, 1).wait_send()
+            copy(owner, 1, 1).wait_send()
+            copy((1 - turb) * count + source, 1, 1).wait_send()
+
+        @pl.when(jnp.logical_and(source <= age, has_above))
+        def _(source=source, owner=owner):
+            copy(owner, 0, 2).wait_send()
+            copy(owner, 1, 2).wait_send()
+            copy((1 - turb) * count + source, 1, 2).wait_send()
+
+
+def reduce_kernel(
+    blocks, stations, grad_rows, early, grads_ref, sums_ref, positions_ref, seed_ref,
+    advected_ref, positions_grad_ref, strengths_grad_ref,
+    work, from_mate, from_below, from_above, late_buf, late_in, halo_out, halo_in,
+    mate_sems, chain_send, chain_recv, late_sems, halo_sems,
+):
+    ages = grads_ref.shape[-1]
+    count = lax.axis_size("age")
+    halo = blocks // stations
+    here, other, below, above, prior, following = place()
+    turb, age, span = here
+    late = grad_rows - early
+    span_rows = early + 2 * late
+    has_below = age > 0
+    has_above = age < count - 1
+
+    def part(column, dest, start, number):
+        owner = column * count + dest
+        return pl.ds(pl.multiple_of(owner * grad_rows + start, 8), number)
+
+    def mate_copy(dest):
+        return pltpu.make_async_remote_copy(
+            src_ref=grads_ref.at[part(1 - turb, dest, 0, early)],
+            dst_ref=from_mate.at[dest],
+            send_sem=mate_sems.at[0, dest],
+            recv_sem=mate_sems.at[1, dest],
+            device_id=other,
+            device_id_type=MESH,
+        )
+
+    def chain_copy(dest, upward):
+        return pltpu.make_async_remote_copy(
+            src_ref=work.at[dest],
+            dst_ref=(from_below if upward else from_above).at[dest],
+            send_sem=chain_send.at[dest],
+            recv_sem=chain_recv.at[0 if upward else 1, dest],
+            device_id=above if upward else below,
+            device_id_type=MESH,
+        )
+
+    greet(count)
+    for distance in range(count - 1, -1, -1):
+        for sign in (1, -1) if distance else (1,):
+            dest = age + sign * distance
+
+            @pl.when(dest < count if sign > 0 else dest >= 0)
+            def _(dest=dest):
+                mate_copy(dest).start()
+
+    def fill(dest):
+        mate_copy(dest).wait_recv()
+        work[dest, pl.ds(0, early), :] = (
+            grads_ref[part(turb, dest, 0, early), :] + from_mate[dest]
+        )
+        work[dest, pl.ds(early, late), :] = grads_ref[part(turb, dest, early, late), :]
+        work[dest, pl.ds(early + late, late), :] = grads_ref[part(1 - turb, dest, early, late), :]
+
+    def add_below(dest):
+        chain_copy(dest, True).wait_recv()
+        work[dest] = work[dest] + from_below[dest]
+
+    def add_above(dest):
+        chain_copy(dest, False).wait_recv()
+        work[dest] = work[dest] + from_above[dest]
+
+    for distance in range(count - 1, 0, -1):
+        up = age + distance
+        down = age - distance
+
+        @pl.when(up < count)
+        def _(dest=up):
+            fill(dest)
+            pl.when(has_below)(lambda: add_below(dest))
+            chain_copy(dest, True).start()
+
+        @pl.when(down >= 0)
+        def _(dest=down):
+            fill(dest)
+            pl.when(has_above)(lambda: add_above(dest))
+            chain_copy(dest, False).start()
+
+    fill(age)
+    pl.when(has_below)(lambda: add_below(age))
+    pl.when(has_above)(lambda: add_above(age))
+    late_buf[...] = work[age, pl.ds(early + late, late), :]
+    late_copy = pltpu.make_async_remote_copy(
+        src_ref=late_buf,
+        dst_ref=late_in,
+        send_sem=late_sems.at[0],
+        recv_sem=late_sems.at[1],
+        device_id=other,
+        device_id_type=MESH,
+    )
+    late_copy.start()
+    advected_ref[...] = positions_ref[...] + time_step * sums_ref[pl.ds(0, 3 * blocks), :]
+    advected_ref[pl.ds(0, blocks), :] = advected_ref[pl.ds(0, blocks), :] + time_step
+    positions_grad_ref[...] = (
+        seed_ref[...] + sums_ref[pl.ds(3 * blocks, 3 * blocks), :] + work[age, pl.ds(0, 3 * blocks), :]
+    )
+    late_copy.wait_recv()
+    work[age, pl.ds(early, late), :] = work[age, pl.ds(early, late), :] + late_in[...]
+    halo_out[...] = work[age, pl.ds(5 * blocks, grad_rows - 5 * blocks), :]
+    halo_copy = pltpu.make_async_remote_copy(
+        src_ref=halo_out,
+        dst_ref=halo_in,
+        send_sem=halo_sems.at[0],
+        recv_sem=halo_sems.at[1],
+        device_id=following,
+        device_id_type=MESH,
+    )
+    halo_copy.start()
+    trail, shed = keeps(stations, ages, (blocks, ages))
+    strengths_grad_ref[pl.ds(0, blocks), :] = work[age, pl.ds(3 * blocks, blocks), :] * trail
+    strengths_grad_ref[pl.ds(blocks, blocks), :] = work[age, pl.ds(4 * blocks, blocks), :] * shed
+    halo_copy.wait_recv()
+    for k in range(3 * halo):
+        at = pl.ds(k * stations, 1)
+        positions_grad_ref[at, :] = positions_grad_ref[at, :] + halo_in[pl.ds(k, 1), :]
+    late_copy.wait_send()
+    halo_copy.wait_send()
+    for dest in range(count):
+        mate_copy(dest).wait_send()
+        pl.when(dest > age)(lambda dest=dest: chain_copy(dest, True).wait_send())
+        pl.when(dest < age)(lambda dest=dest: chain_copy(dest, False).wait_send())
+
+
 def local_dense(positions, strengths, core_radius, adjoint_seed, pair_target, pair_owner, pair_source):
     shape_here = positions.shape
     stations = shape_here[3]
     ages = shape_here[4]
     blocks = shape_here[1] * shape_here[2] * stations
     halo = blocks // stations
-    group = lax.axis_size("turb") * lax.axis_size("age")
+    count = lax.axis_size("age")
+    group = lax.axis_size("turb") * count
     pairs = pair_target.shape[-1]
     per_owner = -(-(6 * blocks + 3 * halo) // 8) * 8
     grad_rows = -(-(5 * blocks + 3 * halo) // 8) * 8
+    early = grad_rows * 5 // 6 // 8 * 8
+    late = grad_rows - early
     target_ids = pair_target.reshape(pairs)
     owner_ids = pair_owner.reshape(pairs)
     source_ids = pair_source.reshape(pairs)
-    age_keep = (
-        lax.axis_index("age") * ages + jnp.arange(ages, dtype=jnp.int32)
-        < ages * lax.axis_size("age") - 1
-    ).astype(jnp.float32)
-    station_keep = (
-        lax.axis_index("span") * stations + jnp.arange(stations, dtype=jnp.int32)
-        < stations * lax.axis_size("span") - 1
-    ).astype(jnp.float32)[:, None]
-    me = lax.axis_index("turb") * lax.axis_size("age") + lax.axis_index("age")
-    next_stations = shifted_2(positions[:, :, :, 0, :], "span", -1)
-    payload = jnp.concatenate(
-        [
-            positions.reshape(3 * blocks, ages),
-            (strengths[0] * age_keep).reshape(blocks, ages),
-            (strengths[1] * station_keep).reshape(blocks, ages),
-            core_radius.reshape(blocks, ages),
-            next_stations.reshape(3 * halo, ages),
-            jnp.zeros((per_owner - 6 * blocks - 3 * halo, ages), jnp.float32),
-        ]
-    )
-    table = lax.all_gather(payload, ("turb", "age"), axis=0, tiled=True)
+    me = lax.axis_index("turb") * count + lax.axis_index("age")
+    vmem = pl.BlockSpec(memory_space=pltpu.VMEM)
+    limit = 40 * 1024 * 1024
+    dma = pltpu.SemaphoreType.DMA
+    rows = positions.reshape(3 * blocks, ages)
+    table = pl.pallas_call(
+        functools.partial(gather_kernel, blocks, stations, per_owner),
+        out_shape=jax.ShapeDtypeStruct((group * per_owner, ages), jnp.float32),
+        in_specs=[vmem] * 3,
+        out_specs=vmem,
+        scratch_shapes=[
+            pltpu.VMEM((per_owner - 6 * blocks, ages), jnp.float32),
+            dma((2,)),
+            dma((3, 2, group)),
+            dma((2, group)),
+        ],
+        compiler_params=pltpu.CompilerParams(
+            collective_id=0, has_side_effects=True, vmem_limit_bytes=limit
+        ),
+    )(rows, strengths.reshape(2 * blocks, ages), core_radius.reshape(blocks, ages))
     station = source_ids % stations
     inner = station < stations - 1
     base = owner_ids * per_owner
@@ -439,8 +754,7 @@
             target_ids,
         ]
     )
-    seed_rows = adjoint_seed.reshape(3 * blocks, ages) * time_step
-    vmem = pl.BlockSpec(memory_space=pltpu.VMEM)
+    seeds = adjoint_seed.reshape(3 * blocks, ages)
     grads, sums = pl.pallas_call(
         functools.partial(pairs_kernel, group, blocks, stations, per_owner, grad_rows),
         out_shape=(
@@ -456,34 +770,50 @@
             pltpu.VMEM(((group * blocks + 1) * SRC_ROWS, ages), jnp.float32),
             pltpu.VMEM((blocks * TGT_ROWS, ages), jnp.float32),
         ],
-        compiler_params=pltpu.CompilerParams(vmem_limit_bytes=40 * 1024 * 1024),
-    )(index, table, seed_rows)
-    mine = lax.psum_scatter(grads, ("turb", "age"), scatter_dimension=0, tiled=True)
-    advected = positions + time_step * sums[: 3 * blocks].reshape(shape_here)
-    advected = advected.at[0].add(time_step)
-    grad_positions = (
-        adjoint_seed
-        + sums[3 * blocks :].reshape(shape_here)
-        + mine[: 3 * blocks].reshape(shape_here)
-    )
-    from_prior = shifted_2(
-        mine[5 * blocks : 5 * blocks + 3 * halo].reshape(shape_here[:3] + (ages,)), "span", 1
-    )
-    grad_positions = grad_positions.at[:, :, :, 0, :].add(from_prior)
-    grad_strengths = mine[3 * blocks : 5 * blocks].reshape(strengths.shape)
-    grad_strengths = grad_strengths * jnp.stack(
-        [
-            jnp.broadcast_to(age_keep[None], (stations, ages)),
-            jnp.broadcast_to(station_keep, (stations, ages)),
-        ]
-    )[:, None, None]
-    return (advected, grad_positions, grad_strengths)
+        compiler_params=pltpu.CompilerParams(vmem_limit_bytes=limit),
+    )(index, table, seeds)
+    extra = grad_rows - 5 * blocks
+    advected, grad_positions, grad_strengths = pl.pallas_call(
+        functools.partial(reduce_kernel, blocks, stations, grad_rows, early),
+        out_shape=(
+            jax.ShapeDtypeStruct((3 * blocks, ages), jnp.float32),
+            jax.ShapeDtypeStruct((3 * blocks, ages), jnp.float32),
+            jax.ShapeDtypeStruct((2 * blocks, ages), jnp.float32),
+        ),
+        in_specs=[vmem] * 4,
+        out_specs=(vmem, vmem, vmem),
+        scratch_shapes=[
+            pltpu.VMEM((count, early + 2 * late, ages), jnp.float32),
+            pltpu.VMEM((count, early, ages), jnp.float32),
+            pltpu.VMEM((count, early + 2 * late, ages), jnp.float32),
+            pltpu.VMEM((count, early + 2 * late, ages), jnp.float32),
+            pltpu.VMEM((late, ages), jnp.float32),
+            pltpu.VMEM((late, ages), jnp.float32),
+            pltpu.VMEM((extra, ages), jnp.float32),
+            pltpu.VMEM((extra, ages), jnp.float32),
+            dma((2, count)),
+            dma((count,)),
+            dma((2, count)),
+            dma((2,)),
+            dma((2,)),
+        ],
+        compiler_params=pltpu.CompilerParams(
+            collective_id=1, has_side_effects=True, vmem_limit_bytes=limit
+        ),
+    )(grads, sums, rows, seeds)
+    return (
+        advected.reshape(shape_here),
+        grad_positions.reshape(shape_here),
+        grad_strengths.reshape(strengths.shape),
+    )
 
 
 def local(positions, strengths, core_radius, adjoint_seed, pair_target, pair_owner, pair_source):
     blocks = positions.shape[1] * positions.shape[2] * positions.shape[3]
     group = lax.axis_size("turb") * lax.axis_size("age")
-    chosen = local_dense if group * blocks <= 8 * pair_target.shape[-1] else local_sparse
+    fits = lax.axis_size("turb") == 2 and lax.axis_size("span") > 2 and lax.axis_size("age") > 1
+    dense = fits and group * blocks <= 8 * pair_target.shape[-1]
+    chosen = local_dense if dense else local_sparse
     return chosen(
         positions, strengths, core_radius, adjoint_seed, pair_target, pair_owner, pair_source
     )

time: 207 us -> 94.4 us (0.46)
  waiting for transfers between devices: 152 us -> 0 us
  Pallas kernels: 17.6 us -> 86.7 us
  between operations: 14.9 us -> 0.69 us
  local copies, waits for them, and re-layouts: 14.3 us -> 5.32 us
  starting transfers between devices: 2.89 us -> 0 us
  other arithmetic: 3.1 us -> 0.74 us
    unnamed x3 -> x0, waiting for transfers between devices: 97.9 us -> none
    pallas_call x0 -> x2, Pallas kernels: none -> 70.2 us  [the longest x1 35.1 us: local_dense(): pl.pallas_call(functools.partial(reduce_kernel, blocks, stations, grad_ro...]
    all_gather x1 -> x0, waiting for transfers between devices: 53.3 us -> none  [local_dense(): table = lax.all_gather(payload, ('turb', 'age'), axis=0, tiled=True)]
    concatenate x1 -> x0, local copies, waits for them, and re-layouts: 6.07 us -> none  [local_dense(): jnp.concatenate([positions.reshape(3 * blocks, ages), (strengths[0] * age...]
    slice x6 -> x0, local copies, waits for them, and re-layouts: 4.29 us -> none  [the longest x1 0.93 us: local_dense(): mine[:3 * blocks].reshape(shape_here)]
    ppermute x2 -> x0, starting transfers between devices: 2.81 us -> none  [shifted_2(): lax.ppermute(value, axis, [(source, source + steps) for source in range(l...]
    unnamed x13 -> x11, local copies, waits for them, and re-layouts: 2.95 us -> 4.56 us
  transfers between devices with their start and end apart: 4 -> 0, of which waited for: 3 -> 0; matrix products, arithmetic and copies ran while one was open for 4% -> 0% of each run, Pallas kernels for 0% -> 0%
where the time goes in v2:
time: 94.4 us; the launch traced here: 93.4 us
  Pallas kernels  86.7 us (92%)
  local copies, waits for them, and re-layouts  5.32 us (6%)
    pallas_call x1, Pallas kernels, local_dense(): pl.pallas_call(functools.partial(reduce_kernel, blocks, stations, grad_ro...  35.1 us
    pallas_call x1, Pallas kernels, local_dense(): pl.pallas_call(functools.partial(gather_kernel, blocks, stations, per_own...  35.1 us
    pallas_call x1, Pallas kernels, local_dense(): pl.pallas_call(functools.partial(pairs_kernel, group, blocks, stations, p...  16.4 us
    unnamed x11, local copies, waits for them, and re-layouts  4.56 us

profile of v2, /device:TPU:0, one launch (start us, length us, event | category | flops | bytes accessed | tf_op | source)
XLA Modules:
  0.0 93.4 jit_solution(1259057052491519022)
XLA Ops:
  0.6 0.0 copy-start
  0.6 0.7 fusion.5
  1.4 0.8 stack.2.index_ref
  2.1 0.0 copy-start.1
  2.2 0.9 copy-done.1
  3.1 0.0 copy-start.2
  3.1 0.9 copy-done.2
  3.9 0.0 copy-start.3
  4.0 0.8 copy-done.3
  4.7 35.1 %shard_map.94.table_ref = f32[4800,128]{1,0:T(8,128)S(1)} custom-call(f32[288,128]{1,0:T(8,128)S(1)} %bitcast.45, f32[192,128]{1,0:T(8,128)S(1)} %bitcast.49, f32[96,128]{1,0:T(8,128)S(1)} %bitcast.51), custom_call_target="tpu_custom_call" | custom-call | tf_op jit(solution)/shard_map/pallas_call | solution.py:727
  39.9 0.0 copy-done
  39.9 16.4 %shard_map.95 = (f32[4032,128]{1,0:T(8,128)S(1)}, f32[576,128]{1,0:T(8,128)S(1)}) custom-call(s32[8,128]{1,0:T(8,128)S(1)} %stack.2.index_ref, f32[4800,128]{1,0:T(8,128)S(1)} %shard_map.94.table_ref, f32[288,128]{1,0:T(8,128)S(1)} %bitcast.43), custom_call_target="tpu_custom_call" | custom-call | tf_op jit(solution)/shard_map/pallas_call | solution.py:758
  56.3 35.1 %shard_map.96 = (f32[288,128]{1,0:T(8,128)S(1)}, f32[288,128]{1,0:T(8,128)S(1)}, f32[192,128]{1,0:T(8,128)S(1)}) custom-call(f32[4032,128]{1,0:T(8,128)S(1)} %get-tuple-element.8.grads_ref, f32[576,128]{1,0:T(8,128)S(1)} %get-tuple-element.9.sums_ref, f32[288,128]{1,0:T(8,128)S(1)} %bitcast.46, f32[288,128]{1,0:T(8,128)S(1)} %bitcast.44), custom_call_target="tpu_custom_call" | custom-call | tf_op jit(solution)/shard_map/pallas_call | solution.py:776
  91.5 0.7 copy.13
  92.1 0.7 copy.14
  92.8 0.6 copy.15
Async XLA Ops:
  0.6 39.2 %copy-start = (f32[3,2,3,16,128]{4,3,2,1,0:T(8,128)S(1)}, f32[3,2,3,16,128]{4,3,2,1,0:T(8,128)}, u32[]{:S(2)}) copy-start(f32[3,2,3,16,128]{4,3,2,1,0:T(8,128)} %param.10) | copy-start | bytes 442372
  2.1 0.9 copy-start.1
  3.1 0.9 copy-start.2
  3.9 0.8 copy-start.3

commit v3 on v2

--- a/solution.py
+++ b/solution.py
@@ -309,10 +309,12 @@
 
 
 def pairs_kernel(
-    group, blocks, stations, per_owner, grad_rows, index_ref, table_ref, seed_ref,
-    grad_ref, out_ref, rows_buf, src_buf, tgt_buf, acc, tgt_acc,
+    group, blocks, stations, per_owner, grad_rows, target_ref, owner_ref, source_ref, table_ref,
+    seed_ref, grad_ref, advected_ref, base_ref, rows_buf, src_buf, tgt_buf, acc, tgt_acc,
 ):
-    pairs = index_ref.shape[1]
+    pairs = target_ref.shape[0]
+    me = lax.axis_index("turb") * lax.axis_size("age") + lax.axis_index("age")
+    own_rows = me * per_owner
     ages = table_ref.shape[-1]
     halo = blocks // stations
     acc[...] = jnp.zeros_like(acc)
@@ -321,12 +323,15 @@
     def tile(t, _):
         for j in range(TILE):
             p = t * TILE + j
-            src = index_ref[0, p]
-            nxt = index_ref[1, p]
-            shed = index_ref[2, p]
-            shed_step = index_ref[3, p]
-            own = index_ref[4, p]
-            tgt = index_ref[5, p]
+            tgt = target_ref[p]
+            owner = owner_ref[p]
+            block = source_ref[p]
+            src = owner * per_owner + block
+            nxt = jnp.where(owner == group - 1, 0, owner + 1) * per_owner + block
+            inner = lax.rem(block, stations) < stations - 1
+            shed = jnp.where(inner, src + 1, owner * per_owner + 6 * blocks + lax.div(block, stations))
+            shed_step = jnp.where(inner, blocks, halo)
+            own = own_rows + tgt
             for r in range(6):
                 rows_buf[pl.ds(r * TILE + j, 1), :] = table_ref[pl.ds(src + r * blocks, 1), :]
             for r in range(3):
@@ -345,17 +350,23 @@
     lax.fori_loop(0, pairs // TILE, tile, 0)
 
     def scatter(p, _):
-        at = pl.ds(pl.multiple_of(index_ref[6, p], SRC_ROWS), SRC_ROWS)
+        at = pl.ds(
+            pl.multiple_of((owner_ref[p] * blocks + source_ref[p] + 1) * SRC_ROWS, SRC_ROWS), SRC_ROWS
+        )
         acc[at, :] += src_buf[pl.ds(pl.multiple_of(p * SRC_ROWS, SRC_ROWS), SRC_ROWS), :]
-        at = pl.ds(pl.multiple_of(index_ref[5, p] * TGT_ROWS, TGT_ROWS), TGT_ROWS)
+        at = pl.ds(pl.multiple_of(target_ref[p] * TGT_ROWS, TGT_ROWS), TGT_ROWS)
         tgt_acc[at, :] += tgt_buf[pl.ds(pl.multiple_of(p * TGT_ROWS, TGT_ROWS), TGT_ROWS), :]
         return 0
 
     lax.fori_loop(0, pairs, scatter, 0, unroll=8)
 
-    for c in range(6):
+    for c in range(3):
         for q in range(0, blocks, 8):
-            out_ref[pl.ds(c * blocks + q, 8), :] = tgt_acc[pl.ds(q * TGT_ROWS + c, 8, stride=TGT_ROWS), :]
+            at = pl.ds(c * blocks + q, 8)
+            velocity = tgt_acc[pl.ds(q * TGT_ROWS + c, 8, stride=TGT_ROWS), :]
+            here = table_ref[pl.ds(pl.multiple_of(own_rows + c * blocks + q, 8), 8), :]
+            advected_ref[at, :] = here + time_step * (velocity + 1.0 if c == 0 else velocity)
+            base_ref[at, :] = seed_ref[at, :] + tgt_acc[pl.ds(q * TGT_ROWS + 3 + c, 8, stride=TGT_ROWS), :]
 
     lane = lax.broadcasted_iota(jnp.int32, (TILE, ages), 1)
     sub = lax.broadcasted_iota(jnp.int32, (TILE, ages), 0)
@@ -437,18 +448,37 @@
 
 def gather_kernel(
     blocks, stations, per_owner, positions_ref, strengths_ref, core_ref, table_ref,
-    halo_buf, halo_sems, send_sems, recv_sems,
+    strengths_buf, halo_buf, load_sems, halo_sems, send_sems, recv_sems,
 ):
     ages = table_ref.shape[-1]
     count = lax.axis_size("age")
     halo = blocks // stations
     here, other, below, above, prior, following = place()
     turb, age, span = here
-    split = 5 * blocks
     me = turb * count + age
     mate = (1 - turb) * count + age
     extra = per_owner - 6 * blocks
-    parts = ((0, split), (split, per_owner - split))
+    parts = (
+        (0, 3 * blocks),
+        (3 * blocks, 2 * blocks),
+        (5 * blocks, per_owner - 5 * blocks),
+    )
+    base = me * per_owner
+    loads = [
+        pltpu.make_async_copy(source, target, load_sems.at[k])
+        for k, (source, target) in enumerate(
+            (
+                (positions_ref, table_ref.at[pl.ds(pl.multiple_of(base, 8), 3 * blocks)]),
+                (strengths_ref, strengths_buf),
+                (core_ref, table_ref.at[pl.ds(pl.multiple_of(base + 5 * blocks, 8), blocks)]),
+            )
+        )
+    ]
+    for load in loads:
+        load.start()
+    halo_buf[...] = jnp.zeros_like(halo_buf)
+    trail, shed = keeps(stations, ages, (blocks, ages))
+    greet(count)
 
     def rows(owner, part):
         return pl.ds(pl.multiple_of(owner * per_owner + parts[part][0], 8), parts[part][1])
@@ -467,20 +497,23 @@
     def arrive(owner, part):
         copy(owner, part, 0).wait_recv()
 
-    base = me * per_owner
-    halo_buf[...] = jnp.zeros_like(halo_buf)
+    has_below = age > 0
+    has_above = age < count - 1
+
+    def share(owner, part):
+        @pl.when(has_below)
+        def _():
+            copy(owner, part, 1).start()
+
+        @pl.when(has_above)
+        def _():
+            copy(owner, part, 2).start()
+
+    loads[0].wait()
+    share(me, 0)
+    copy(me, 0, 0).start()
     for k in range(3 * halo):
-        halo_buf[pl.ds(k, 1), :] = positions_ref[pl.ds(k * stations, 1), :]
-    table_ref[pl.ds(pl.multiple_of(base, 8), 3 * blocks), :] = positions_ref[...]
-    trail, shed = keeps(stations, ages, (blocks, ages))
-    table_ref[pl.ds(pl.multiple_of(base + 3 * blocks, 8), blocks), :] = (
-        strengths_ref[pl.ds(0, blocks), :] * trail
-    )
-    table_ref[pl.ds(pl.multiple_of(base + 4 * blocks, 8), blocks), :] = (
-        strengths_ref[pl.ds(blocks, blocks), :] * shed
-    )
-    table_ref[pl.ds(pl.multiple_of(base + 5 * blocks, 8), blocks), :] = core_ref[...]
-    greet(count)
+        halo_buf[pl.ds(k, 1), :] = table_ref[pl.ds(base + k * stations, 1), :]
     halo_copy = pltpu.make_async_remote_copy(
         src_ref=halo_buf,
         dst_ref=table_ref.at[pl.ds(pl.multiple_of(base + 6 * blocks, 8), extra)],
@@ -490,97 +523,65 @@
         device_id_type=MESH,
     )
     halo_copy.start()
-
-    has_below = age > 0
-    has_above = age < count - 1
-
-    @pl.when(has_below)
-    def _():
-        copy(me, 0, 1).start()
-
-    @pl.when(has_above)
-    def _():
-        copy(me, 0, 2).start()
-
-    copy(me, 0, 0).start()
+    loads[1].wait()
+    table_ref[pl.ds(pl.multiple_of(base + 3 * blocks, 8), blocks), :] = (
+        strengths_buf[pl.ds(0, blocks), :] * trail
+    )
+    table_ref[pl.ds(pl.multiple_of(base + 4 * blocks, 8), blocks), :] = (
+        strengths_buf[pl.ds(blocks, blocks), :] * shed
+    )
+    share(me, 1)
+    copy(me, 1, 0).start()
+    loads[2].wait()
     halo_copy.wait_recv()
-    copy(me, 1, 0).start()
-
-    @pl.when(has_below)
-    def _():
-        copy(me, 1, 1).start()
-
-    @pl.when(has_above)
-    def _():
-        copy(me, 1, 2).start()
-
-    arrive(mate, 1)
-
-    @pl.when(has_below)
-    def _():
-        copy(mate, 1, 1).start()
-
-    @pl.when(has_above)
-    def _():
-        copy(mate, 1, 2).start()
-
+    copy(me, 2, 0).start()
+    share(me, 2)
+    arrive(mate, 2)
+    share(mate, 2)
     for step in range(1, count):
-        for way, sign in ((2, -1), (1, 1)):
-            source = age + sign * step
-            exists = source >= 0 if sign < 0 else source < count
-            onward = has_above if way == 2 else has_below
-
-            @pl.when(exists)
-            def _(source=source, way=way, onward=onward):
-                owner = turb * count + source
-                arrive(owner, 0)
-
-                @pl.when(onward)
-                def _():
-                    copy(owner, 0, way).start()
-
-                copy(owner, 0, 0).start()
-
-        for way, sign in ((2, -1), (1, 1)):
-            source = age + sign * step
-            exists = source >= 0 if sign < 0 else source < count
-            onward = has_above if way == 2 else has_below
-
-            @pl.when(exists)
-            def _(source=source, way=way, onward=onward):
-                for column in (turb, 1 - turb):
-                    owner = column * count + source
-                    arrive(owner, 1)
-
-                    @pl.when(onward)
-                    def _(owner=owner):
-                        copy(owner, 1, way).start()
+        for part in range(3):
+            for way, sign in ((2, -1), (1, 1)):
+                source = age + sign * step
+                onward = has_above if way == 2 else has_below
+
+                @pl.when(source >= 0 if sign < 0 else source < count)
+                def _(source=source, way=way, onward=onward, part=part):
+                    for column in (turb, 1 - turb)[: 2 if part == 2 else 1]:
+                        owner = column * count + source
+                        arrive(owner, part)
+
+                        @pl.when(onward)
+                        def _(owner=owner):
+                            copy(owner, part, way).start()
+
+                        if part < 2:
+                            copy(owner, part, 0).start()
 
     for source in range(count):
-        arrive((1 - turb) * count + source, 0)
+        for part in range(2):
+            arrive((1 - turb) * count + source, part)
     halo_copy.wait_send()
-    copy(me, 1, 0).wait_send()
+    copy(me, 2, 0).wait_send()
     for source in range(count):
-        owner = turb * count + source
-        copy(owner, 0, 0).wait_send()
+        sent = [(turb * count + source, part) for part in range(3)]
+        sent.append(((1 - turb) * count + source, 2))
+        for part in range(2):
+            copy(sent[part][0], part, 0).wait_send()
 
         @pl.when(jnp.logical_and(source >= age, has_below))
-        def _(source=source, owner=owner):
-            copy(owner, 0, 1).wait_send()
-            copy(owner, 1, 1).wait_send()
-            copy((1 - turb) * count + source, 1, 1).wait_send()
+        def _(sent=sent):
+            for owner, part in sent:
+                copy(owner, part, 1).wait_send()
 
         @pl.when(jnp.logical_and(source <= age, has_above))
-        def _(source=source, owner=owner):
-            copy(owner, 0, 2).wait_send()
-            copy(owner, 1, 2).wait_send()
-            copy((1 - turb) * count + source, 1, 2).wait_send()
+        def _(sent=sent):
+            for owner, part in sent:
+                copy(owner, part, 2).wait_send()
 
 
 def reduce_kernel(
-    blocks, stations, grad_rows, early, grads_ref, sums_ref, positions_ref, seed_ref,
-    advected_ref, positions_grad_ref, strengths_grad_ref,
-    work, from_mate, from_below, from_above, late_buf, late_in, halo_out, halo_in,
+    blocks, stations, grad_rows, early, grads_ref, base_ref, positions_grad_ref, strengths_grad_ref,
+    work, from_mate, from_below, from_above, late_in, halo_out, halo_in,
     mate_sems, chain_send, chain_recv, late_sems, halo_sems,
 ):
     ages = grads_ref.shape[-1]
@@ -589,7 +590,10 @@
     here, other, below, above, prior, following = place()
     turb, age, span = here
     late = grad_rows - early
-    span_rows = early + 2 * late
+    half = (early + 2 * late) // 16 * 8
+    cut = half - 2 * late
+    pieces = ((0, cut), (cut, early - cut))
+    spans = ((0, half), (half, early + 2 * late - half))
     has_below = age > 0
     has_above = age < count - 1
 
@@ -597,73 +601,73 @@
         owner = column * count + dest
         return pl.ds(pl.multiple_of(owner * grad_rows + start, 8), number)
 
-    def mate_copy(dest):
+    def mate_copy(dest, piece):
         return pltpu.make_async_remote_copy(
-            src_ref=grads_ref.at[part(1 - turb, dest, 0, early)],
-            dst_ref=from_mate.at[dest],
-            send_sem=mate_sems.at[0, dest],
-            recv_sem=mate_sems.at[1, dest],
+            src_ref=grads_ref.at[part(1 - turb, dest, *pieces[piece])],
+            dst_ref=from_mate.at[dest, pl.ds(*pieces[piece])],
+            send_sem=mate_sems.at[0, dest, piece],
+            recv_sem=mate_sems.at[1, dest, piece],
             device_id=other,
             device_id_type=MESH,
         )
 
-    def chain_copy(dest, upward):
+    def chain_copy(dest, piece, upward):
+        at = pl.ds(*spans[piece])
         return pltpu.make_async_remote_copy(
-            src_ref=work.at[dest],
-            dst_ref=(from_below if upward else from_above).at[dest],
-            send_sem=chain_send.at[dest],
-            recv_sem=chain_recv.at[0 if upward else 1, dest],
+            src_ref=work.at[dest, at],
+            dst_ref=(from_below if upward else from_above).at[dest, at],
+            send_sem=chain_send.at[dest, piece],
+            recv_sem=chain_recv.at[0 if upward else 1, dest, piece],
             device_id=above if upward else below,
             device_id_type=MESH,
         )
 
-    greet(count)
+    order = [jnp.int32(0)] * count
+    rank = jnp.int32(0)
     for distance in range(count - 1, -1, -1):
         for sign in (1, -1) if distance else (1,):
             dest = age + sign * distance
-
-            @pl.when(dest < count if sign > 0 else dest >= 0)
-            def _(dest=dest):
-                mate_copy(dest).start()
-
-    def fill(dest):
-        mate_copy(dest).wait_recv()
-        work[dest, pl.ds(0, early), :] = (
-            grads_ref[part(turb, dest, 0, early), :] + from_mate[dest]
+            valid = jnp.logical_and(dest >= 0, dest < count)
+            order = [
+                jnp.where(jnp.logical_and(valid, rank == k), dest, order[k]) for k in range(count)
+            ]
+            rank = rank + valid.astype(jnp.int32)
+    steps = [(order[k], piece) for k in range(count) for piece in range(2)]
+
+    greet(count)
+    mate_copy(*steps[0]).start()
+
+    def take(number):
+        dest, piece = steps[number]
+        mate_copy(dest, piece).wait_recv()
+        if number + 1 < len(steps):
+            mate_copy(*steps[number + 1]).start()
+        start, size = pieces[piece]
+        if piece == 0:
+            work[dest, pl.ds(0, late), :] = grads_ref[part(turb, dest, early, late), :]
+            work[dest, pl.ds(late, late), :] = grads_ref[part(1 - turb, dest, early, late), :]
+        work[dest, pl.ds(2 * late + start, size), :] = (
+            grads_ref[part(turb, dest, start, size), :] + from_mate[dest, pl.ds(start, size), :]
         )
-        work[dest, pl.ds(early, late), :] = grads_ref[part(turb, dest, early, late), :]
-        work[dest, pl.ds(early + late, late), :] = grads_ref[part(1 - turb, dest, early, late), :]
-
-    def add_below(dest):
-        chain_copy(dest, True).wait_recv()
-        work[dest] = work[dest] + from_below[dest]
-
-    def add_above(dest):
-        chain_copy(dest, False).wait_recv()
-        work[dest] = work[dest] + from_above[dest]
-
-    for distance in range(count - 1, 0, -1):
-        up = age + distance
-        down = age - distance
-
-        @pl.when(up < count)
-        def _(dest=up):
-            fill(dest)
-            pl.when(has_below)(lambda: add_below(dest))
-            chain_copy(dest, True).start()
-
-        @pl.when(down >= 0)
-        def _(dest=down):
-            fill(dest)
-            pl.when(has_above)(lambda: add_above(dest))
-            chain_copy(dest, False).start()
-
-    fill(age)
-    pl.when(has_below)(lambda: add_below(age))
-    pl.when(has_above)(lambda: add_above(age))
-    late_buf[...] = work[age, pl.ds(early + late, late), :]
+        at = pl.ds(*spans[piece])
+
+        @pl.when(jnp.logical_and(dest >= age, has_below))
+        def _():
+            chain_copy(dest, piece, True).wait_recv()
+            work[dest, at, :] = work[dest, at, :] + from_below[dest, at, :]
+
+        @pl.when(jnp.logical_and(dest <= age, has_above))
+        def _():
+            chain_copy(dest, piece, False).wait_recv()
+            work[dest, at, :] = work[dest, at, :] + from_above[dest, at, :]
+
+        pl.when(dest > age)(lambda: chain_copy(dest, piece, True).start())
+        pl.when(dest < age)(lambda: chain_copy(dest, piece, False).start())
+
+    for number in range(len(steps) - 1):
+        take(number)
     late_copy = pltpu.make_async_remote_copy(
-        src_ref=late_buf,
+        src_ref=work.at[age, pl.ds(late, late)],
         dst_ref=late_in,
         send_sem=late_sems.at[0],
         recv_sem=late_sems.at[1],
@@ -671,14 +675,9 @@
         device_id_type=MESH,
     )
     late_copy.start()
-    advected_ref[...] = positions_ref[...] + time_step * sums_ref[pl.ds(0, 3 * blocks), :]
-    advected_ref[pl.ds(0, blocks), :] = advected_ref[pl.ds(0, blocks), :] + time_step
-    positions_grad_ref[...] = (
-        seed_ref[...] + sums_ref[pl.ds(3 * blocks, 3 * blocks), :] + work[age, pl.ds(0, 3 * blocks), :]
-    )
     late_copy.wait_recv()
-    work[age, pl.ds(early, late), :] = work[age, pl.ds(early, late), :] + late_in[...]
-    halo_out[...] = work[age, pl.ds(5 * blocks, grad_rows - 5 * blocks), :]
+    work[age, pl.ds(0, late), :] = work[age, pl.ds(0, late), :] + late_in[...]
+    halo_out[...] = work[age, pl.ds(5 * blocks - early, grad_rows - 5 * blocks), :]
     halo_copy = pltpu.make_async_remote_copy(
         src_ref=halo_out,
         dst_ref=halo_in,
@@ -688,9 +687,18 @@
         device_id_type=MESH,
     )
     halo_copy.start()
-    trail, shed = keeps(stations, ages, (blocks, ages))
-    strengths_grad_ref[pl.ds(0, blocks), :] = work[age, pl.ds(3 * blocks, blocks), :] * trail
-    strengths_grad_ref[pl.ds(blocks, blocks), :] = work[age, pl.ds(4 * blocks, blocks), :] * shed
+    trail, shed = keeps(stations, ages, (2 * blocks, ages))
+    row = lax.broadcasted_iota(jnp.int32, (2 * blocks, ages), 0)
+    keep = jnp.where(row < blocks, trail, shed)
+    first = early - 3 * blocks
+    strengths_grad_ref[pl.ds(first, 2 * blocks - first), :] = (
+        work[age, pl.ds(0, 2 * blocks - first), :] * keep[first:]
+    )
+    take(len(steps) - 1)
+    strengths_grad_ref[pl.ds(0, first), :] = (
+        work[age, pl.ds(2 * late + 3 * blocks, first), :] * keep[:first]
+    )
+    positions_grad_ref[...] = base_ref[...] + work[age, pl.ds(2 * late, 3 * blocks), :]
     halo_copy.wait_recv()
     for k in range(3 * halo):
         at = pl.ds(k * stations, 1)
@@ -698,9 +706,10 @@
     late_copy.wait_send()
     halo_copy.wait_send()
     for dest in range(count):
-        mate_copy(dest).wait_send()
-        pl.when(dest > age)(lambda dest=dest: chain_copy(dest, True).wait_send())
-        pl.when(dest < age)(lambda dest=dest: chain_copy(dest, False).wait_send())
+        for piece in range(2):
+            mate_copy(dest, piece).wait_send()
+            pl.when(dest > age)(lambda d=dest, p=piece: chain_copy(d, p, True).wait_send())
+            pl.when(dest < age)(lambda d=dest, p=piece: chain_copy(d, p, False).wait_send())
 
 
 def local_dense(positions, strengths, core_radius, adjoint_seed, pair_target, pair_owner, pair_source):
@@ -716,10 +725,6 @@
     grad_rows = -(-(5 * blocks + 3 * halo) // 8) * 8
     early = grad_rows * 5 // 6 // 8 * 8
     late = grad_rows - early
-    target_ids = pair_target.reshape(pairs)
-    owner_ids = pair_owner.reshape(pairs)
-    source_ids = pair_source.reshape(pairs)
-    me = lax.axis_index("turb") * count + lax.axis_index("age")
     vmem = pl.BlockSpec(memory_space=pltpu.VMEM)
     limit = 40 * 1024 * 1024
     dma = pltpu.SemaphoreType.DMA
@@ -727,42 +732,32 @@
     table = pl.pallas_call(
         functools.partial(gather_kernel, blocks, stations, per_owner),
         out_shape=jax.ShapeDtypeStruct((group * per_owner, ages), jnp.float32),
-        in_specs=[vmem] * 3,
+        in_specs=[pl.BlockSpec(memory_space=pl.ANY)] * 3,
         out_specs=vmem,
         scratch_shapes=[
+            pltpu.VMEM((2 * blocks, ages), jnp.float32),
             pltpu.VMEM((per_owner - 6 * blocks, ages), jnp.float32),
+            dma((3,)),
             dma((2,)),
-            dma((3, 2, group)),
-            dma((2, group)),
+            dma((3, 3, group)),
+            dma((3, group)),
         ],
         compiler_params=pltpu.CompilerParams(
             collective_id=0, has_side_effects=True, vmem_limit_bytes=limit
         ),
     )(rows, strengths.reshape(2 * blocks, ages), core_radius.reshape(blocks, ages))
-    station = source_ids % stations
-    inner = station < stations - 1
-    base = owner_ids * per_owner
-    index = jnp.stack(
-        [
-            base + source_ids,
-            (owner_ids + 1) % group * per_owner + source_ids,
-            base + jnp.where(inner, source_ids + 1, 6 * blocks + source_ids // stations),
-            jnp.where(inner, blocks, halo),
-            me * per_owner + target_ids,
-            target_ids,
-            (owner_ids * blocks + source_ids + 1) * SRC_ROWS,
-            target_ids,
-        ]
-    )
     seeds = adjoint_seed.reshape(3 * blocks, ages)
-    grads, sums = pl.pallas_call(
+    smem = pl.BlockSpec(memory_space=pltpu.SMEM)
+    rows_out = jax.ShapeDtypeStruct((3 * blocks, ages), jnp.float32)
+    grads, advected, grad_base = pl.pallas_call(
         functools.partial(pairs_kernel, group, blocks, stations, per_owner, grad_rows),
         out_shape=(
             jax.ShapeDtypeStruct((group * grad_rows, ages), jnp.float32),
-            jax.ShapeDtypeStruct((6 * blocks, ages), jnp.float32),
+            rows_out,
+            rows_out,
         ),
-        in_specs=[pl.BlockSpec(memory_space=pltpu.SMEM), vmem, vmem],
-        out_specs=(vmem, vmem),
+        in_specs=[smem, smem, smem, vmem, vmem],
+        out_specs=(vmem, vmem, vmem),
         scratch_shapes=[
             pltpu.VMEM((18 * TILE, ages), jnp.float32),
             pltpu.VMEM((pairs * SRC_ROWS, ages), jnp.float32),
@@ -771,36 +766,37 @@
             pltpu.VMEM((blocks * TGT_ROWS, ages), jnp.float32),
         ],
         compiler_params=pltpu.CompilerParams(vmem_limit_bytes=limit),
-    )(index, table, seeds)
+    )(
+        pair_target.reshape(pairs),
+        pair_owner.reshape(pairs),
+        pair_source.reshape(pairs),
+        table,
+        seeds,
+    )
     extra = grad_rows - 5 * blocks
-    advected, grad_positions, grad_strengths = pl.pallas_call(
+    grad_positions, grad_strengths = pl.pallas_call(
         functools.partial(reduce_kernel, blocks, stations, grad_rows, early),
-        out_shape=(
-            jax.ShapeDtypeStruct((3 * blocks, ages), jnp.float32),
-            jax.ShapeDtypeStruct((3 * blocks, ages), jnp.float32),
-            jax.ShapeDtypeStruct((2 * blocks, ages), jnp.float32),
-        ),
-        in_specs=[vmem] * 4,
-        out_specs=(vmem, vmem, vmem),
+        out_shape=(rows_out, jax.ShapeDtypeStruct((2 * blocks, ages), jnp.float32)),
+        in_specs=[vmem] * 2,
+        out_specs=(vmem, vmem),
         scratch_shapes=[
             pltpu.VMEM((count, early + 2 * late, ages), jnp.float32),
             pltpu.VMEM((count, early, ages), jnp.float32),
             pltpu.VMEM((count, early + 2 * late, ages), jnp.float32),
             pltpu.VMEM((count, early + 2 * late, ages), jnp.float32),
             pltpu.VMEM((late, ages), jnp.float32),
-            pltpu.VMEM((late, ages), jnp.float32),
             pltpu.VMEM((extra, ages), jnp.float32),
             pltpu.VMEM((extra, ages), jnp.float32),
-            dma((2, count)),
-            dma((count,)),
-            dma((2, count)),
+            dma((2, count, 2)),
+            dma((count, 2)),
+            dma((2, count, 2)),
             dma((2,)),
             dma((2,)),
         ],
         compiler_params=pltpu.CompilerParams(
             collective_id=1, has_side_effects=True, vmem_limit_bytes=limit
         ),
-    )(grads, sums, rows, seeds)
+    )(grads, grad_base)
     return (
         advected.reshape(shape_here),
         grad_positions.reshape(shape_here),

time: 94.4 us -> 91.2 us (0.966)
  local copies, waits for them, and re-layouts: 5.32 us -> 3.93 us
    pallas_call x1, Pallas kernels: 35.1 us -> 34.1 us  [local_dense(): pl.pallas_call(functools.partial(gather_kernel, blocks, stations, per_own...]
    unnamed x11 -> x16, local copies, waits for them, and re-layouts: 4.56 us -> 3.93 us
where the time goes in v3:
time: 91.2 us; the launch traced here: 90.6 us
  Pallas kernels  86 us (94%)
  local copies, waits for them, and re-layouts  3.93 us (4%)
    pallas_call x1, Pallas kernels, local_dense(): pl.pallas_call(functools.partial(reduce_kernel, blocks, stations, grad_ro...  35 us
    pallas_call x1, Pallas kernels, local_dense(): pl.pallas_call(functools.partial(gather_kernel, blocks, stations, per_own...  34.1 us
    pallas_call x1, Pallas kernels, local_dense(): pl.pallas_call(functools.partial(pairs_kernel, group, blocks, stations, p...  17 us
    unnamed x16, local copies, waits for them, and re-layouts  3.93 us

profile of v3, /device:TPU:0, one launch (start us, length us, event | category | flops | bytes accessed | tf_op | source)
XLA Modules:
  0.0 90.6 jit_solution(15245366098088279871)
XLA Ops:
  0.6 0.0 copy-start.6
  0.6 0.0 copy-start.5
  0.7 0.0 copy-start.4
  0.7 0.0 copy-start
  0.7 0.9 %copy-done = f32[3,2,3,16,128]{4,3,2,1,0:T(8,128)S(1)} copy-done((f32[3,2,3,16,128]{4,3,2,1,0:T(8,128)S(1)}, f32[3,2,3,16,128]{4,3,2,1,0:T(8,128)}, u32[]{:S(2)}) %copy-start) | copy-done | bytes 147480
  1.6 0.0 copy-start.2
  1.6 0.9 copy-done.2
  2.5 0.0 copy-start.3
  2.5 0.8 copy-done.3
  3.3 0.0 copy-start.1
  3.3 34.1 %shard_map.94.table_ref = f32[4800,128]{1,0:T(8,128)S(1)} custom-call(f32[288,128]{1,0:T(8,128)S(1)} %bitcast.11, f32[192,128]{1,0:T(8,128)S(1)} %bitcast.13, f32[96,128]{1,0:T(8,128)S(1)} %bitcast.15), custom_call_target="tpu_custom_call" | custom-call | tf_op jit(solution)/shard_map/pallas_call | solution.py:732
  37.4 0.0 copy-done.6
  37.4 0.0 copy-done.5
  37.4 0.0 copy-done.4
  37.4 0.0 copy-done.1
  37.4 17.0 %shard_map.95 = (f32[4032,128]{1,0:T(8,128)S(1)}, f32[288,128]{1,0:T(8,128)}, f32[288,128]{1,0:T(8,128)S(1)}) custom-call(s32[128]{0:T(128)S(1)} %bitcast.16, s32[128]{0:T(128)S(1)} %bitcast.17, s32[128]{0:T(128)S(1)} %bitcast.18, f32[4800,128]{1,0:T(8,128)S(1)} %shard_map.94.table_ref, f32[288,128]{1,0:T(8,128)S(1)} %bitcast.12), custom_call_target="tpu_custom_call" | custom-call | tf_op jit(solution)/shard_map/pallas_call | solution.py:752
  54.4 35.0 %shard_map.96 = (f32[288,128]{1,0:T(8,128)S(1)}, f32[192,128]{1,0:T(8,128)S(1)}) custom-call(f32[4032,128]{1,0:T(8,128)S(1)} %get-tuple-element.9.grads_ref, f32[288,128]{1,0:T(8,128)S(1)} %get-tuple-element.10.base_ref), custom_call_target="tpu_custom_call" | custom-call | tf_op jit(solution)/shard_map/pallas_call | solution.py:777
  89.3 0.7 copy.12
  90.0 0.6 copy.13
Async XLA Ops:
  0.6 36.7 %copy-start.6 = (s32[1,1,1,128]{3,2,1,0:T(1,128)S(1)}, s32[1,1,1,128]{3,2,1,0:T(1,128)}, u32[]{:S(2)}) copy-start(s32[1,1,1,128]{3,2,1,0:T(1,128)} %param.13) | copy-start | bytes 1540
  0.6 36.7 %copy-start.5 = (s32[1,1,1,128]{3,2,1,0:T(1,128)S(1)}, s32[1,1,1,128]{3,2,1,0:T(1,128)}, u32[]{:S(2)}) copy-start(s32[1,1,1,128]{3,2,1,0:T(1,128)} %param.12) | copy-start | bytes 1540
  0.7 36.7 %copy-start.4 = (s32[1,1,1,128]{3,2,1,0:T(1,128)S(1)}, s32[1,1,1,128]{3,2,1,0:T(1,128)}, u32[]{:S(2)}) copy-start(s32[1,1,1,128]{3,2,1,0:T(1,128)} %param.11) | copy-start | bytes 1540
  0.7 0.9 %copy-start = (f32[3,2,3,16,128]{4,3,2,1,0:T(8,128)S(1)}, f32[3,2,3,16,128]{4,3,2,1,0:T(8,128)}, u32[]{:S(2)}) copy-start(f32[3,2,3,16,128]{4,3,2,1,0:T(8,128)} %param.7) | copy-start | bytes 442372
  1.6 0.9 copy-start.2
  2.5 0.8 copy-start.3
  3.3 34.1 %copy-start.1 = (f32[3,2,3,16,128]{4,3,2,1,0:T(8,128)S(1)}, f32[3,2,3,16,128]{4,3,2,1,0:T(8,128)}, u32[]{:S(2)}) copy-start(f32[3,2,3,16,128]{4,3,2,1,0:T(8,128)} %param.10) | copy-start | bytes 442372

commit v4 on v3

--- a/solution.py
+++ b/solution.py
@@ -636,12 +636,13 @@
 
     greet(count)
     mate_copy(*steps[0]).start()
+    mate_copy(*steps[1]).start()
 
     def take(number):
         dest, piece = steps[number]
         mate_copy(dest, piece).wait_recv()
-        if number + 1 < len(steps):
-            mate_copy(*steps[number + 1]).start()
+        if number + 2 < len(steps):
+            mate_copy(*steps[number + 2]).start()
         start, size = pieces[piece]
         if piece == 0:
             work[dest, pl.ds(0, late), :] = grads_ref[part(turb, dest, early, late), :]

time: 91.2 us -> 85.4 us (0.936)
  Pallas kernels: 86 us -> 80.5 us
    pallas_call x1, Pallas kernels: 35 us -> 29.5 us  [local_dense(): pl.pallas_call(functools.partial(reduce_kernel, blocks, stations, grad_ro...]
where the time goes in v4:
time: 85.4 us; the launch traced here: 85.2 us
  Pallas kernels  80.5 us (94%)
  local copies, waits for them, and re-layouts  3.93 us (5%)
    pallas_call x1, Pallas kernels, local_dense(): pl.pallas_call(functools.partial(gather_kernel, blocks, stations, per_own...  34.1 us
    pallas_call x1, Pallas kernels, local_dense(): pl.pallas_call(functools.partial(reduce_kernel, blocks, stations, grad_ro...  29.5 us
    pallas_call x1, Pallas kernels, local_dense(): pl.pallas_call(functools.partial(pairs_kernel, group, blocks, stations, p...  17 us
    unnamed x16, local copies, waits for them, and re-layouts  3.93 us

profile of v4, /device:TPU:0, one launch (start us, length us, event | category | flops | bytes accessed | tf_op | source)
XLA Modules:
  0.0 85.2 jit_solution(12745352374407906249)
XLA Ops:
  0.6 0.0 copy-start.6
  0.6 0.0 copy-start.5
  0.7 0.0 copy-start.4
  0.7 0.0 copy-start
  0.7 0.9 %copy-done = f32[3,2,3,16,128]{4,3,2,1,0:T(8,128)S(1)} copy-done((f32[3,2,3,16,128]{4,3,2,1,0:T(8,128)S(1)}, f32[3,2,3,16,128]{4,3,2,1,0:T(8,128)}, u32[]{:S(2)}) %copy-start) | copy-done | bytes 147480
  1.6 0.0 copy-start.2
  1.6 0.9 %copy-done.2 = f32[2,2,3,16,128]{4,3,2,1,0:T(8,128)S(1)} copy-done((f32[2,2,3,16,128]{4,3,2,1,0:T(8,128)S(1)}, f32[2,2,3,16,128]{4,3,2,1,0:T(8,128)}, u32[]{:S(2)}) %copy-start.2) | copy-done | bytes 98328
  2.5 0.0 copy-start.3
  2.5 0.8 copy-done.3
  3.3 0.0 copy-start.1
  3.3 34.1 %shard_map.94.table_ref = f32[4800,128]{1,0:T(8,128)S(1)} custom-call(f32[288,128]{1,0:T(8,128)S(1)} %bitcast.11, f32[192,128]{1,0:T(8,128)S(1)} %bitcast.13, f32[96,128]{1,0:T(8,128)S(1)} %bitcast.15), custom_call_target="tpu_custom_call" | custom-call | tf_op jit(solution)/shard_map/pallas_call | solution.py:733
  37.4 0.0 copy-done.6
  37.4 0.0 copy-done.5
  37.4 0.0 copy-done.4
  37.4 0.0 copy-done.1
  37.4 17.0 %shard_map.95 = (f32[4032,128]{1,0:T(8,128)S(1)}, f32[288,128]{1,0:T(8,128)}, f32[288,128]{1,0:T(8,128)S(1)}) custom-call(s32[128]{0:T(128)S(1)} %bitcast.16, s32[128]{0:T(128)S(1)} %bitcast.17, s32[128]{0:T(128)S(1)} %bitcast.18, f32[4800,128]{1,0:T(8,128)S(1)} %shard_map.94.table_ref, f32[288,128]{1,0:T(8,128)S(1)} %bitcast.12), custom_call_target="tpu_custom_call" | custom-call | tf_op jit(solution)/shard_map/pallas_call | solution.py:753
  54.4 29.5 %shard_map.96 = (f32[288,128]{1,0:T(8,128)S(1)}, f32[192,128]{1,0:T(8,128)S(1)}) custom-call(f32[4032,128]{1,0:T(8,128)S(1)} %get-tuple-element.9.grads_ref, f32[288,128]{1,0:T(8,128)S(1)} %get-tuple-element.10.base_ref), custom_call_target="tpu_custom_call" | custom-call | tf_op jit(solution)/shard_map/pallas_call | solution.py:778
  83.9 0.7 copy.12
  84.5 0.6 copy.13
Async XLA Ops:
  0.6 36.7 %copy-start.6 = (s32[1,1,1,128]{3,2,1,0:T(1,128)S(1)}, s32[1,1,1,128]{3,2,1,0:T(1,128)}, u32[]{:S(2)}) copy-start(s32[1,1,1,128]{3,2,1,0:T(1,128)} %param.13) | copy-start | bytes 1540
  0.6 36.7 %copy-start.5 = (s32[1,1,1,128]{3,2,1,0:T(1,128)S(1)}, s32[1,1,1,128]{3,2,1,0:T(1,128)}, u32[]{:S(2)}) copy-start(s32[1,1,1,128]{3,2,1,0:T(1,128)} %param.12) | copy-start | bytes 1540
  0.7 36.7 %copy-start.4 = (s32[1,1,1,128]{3,2,1,0:T(1,128)S(1)}, s32[1,1,1,128]{3,2,1,0:T(1,128)}, u32[]{:S(2)}) copy-start(s32[1,1,1,128]{3,2,1,0:T(1,128)} %param.11) | copy-start | bytes 1540
  0.7 0.9 %copy-start = (f32[3,2,3,16,128]{4,3,2,1,0:T(8,128)S(1)}, f32[3,2,3,16,128]{4,3,2,1,0:T(8,128)}, u32[]{:S(2)}) copy-start(f32[3,2,3,16,128]{4,3,2,1,0:T(8,128)} %param.7) | copy-start | bytes 442372
  1.6 0.9 %copy-start.2 = (f32[2,2,3,16,128]{4,3,2,1,0:T(8,128)S(1)}, f32[2,2,3,16,128]{4,3,2,1,0:T(8,128)}, u32[]{:S(2)}) copy-start(f32[2,2,3,16,128]{4,3,2,1,0:T(8,128)} %param.8) | copy-start | bytes 294916
  2.5 0.8 copy-start.3
  3.3 34.1 %copy-start.1 = (f32[3,2,3,16,128]{4,3,2,1,0:T(8,128)S(1)}, f32[3,2,3,16,128]{4,3,2,1,0:T(8,128)}, u32[]{:S(2)}) copy-start(f32[3,2,3,16,128]{4,3,2,1,0:T(8,128)} %param.10) | copy-start | bytes 442372

commit v5 on v4

--- a/solution.py
+++ b/solution.py
@@ -206,8 +206,6 @@
 
 
 TILE = 8
-SRC_ROWS = 16
-TGT_ROWS = 8
 
 
 def cross(a, b):
@@ -303,22 +301,237 @@
         back = (-offset) % ages
         both = vel + g1
         out = [out[i] + (pltpu.roll(both[i], back, 1) if back else both[i]) for i in range(6)]
-    grad_begin = [-(sum_r1[i] + sum_r0[0][i] + sum_r0[1][i]) for i in range(3)]
-    grad_source = grad_begin + sum_r0[0] + sum_r0[1] + [g * (1.0 / four_pi) for g in sum_gamma]
-    return grad_source, out
-
-
-def pairs_kernel(
-    group, blocks, stations, per_owner, grad_rows, target_ref, owner_ref, source_ref, table_ref,
-    seed_ref, grad_ref, advected_ref, base_ref, rows_buf, src_buf, tgt_buf, acc, tgt_acc,
+    carry = zero
+    grad_begin = []
+    for i in range(3):
+        moved = pltpu.roll(sum_r0[0][i], 1, 1)
+        carry = jnp.where(lane == i, pltpu.roll(moved, i, 1) if i else moved, carry)
+        moved = jnp.where(lane == 0, 0.0, moved)
+        grad_begin.append(moved - (sum_r1[i] + sum_r0[0][i] + sum_r0[1][i]))
+    gammas = [g * (1.0 / four_pi) for g in sum_gamma]
+    return grad_begin + gammas + sum_r0[1] + [carry] + out
+
+
+MESH = pl.DeviceIdType.MESH
+
+
+def place():
+    here = (lax.axis_index("turb"), lax.axis_index("age"), lax.axis_index("span"))
+    spans = lax.axis_size("span")
+    turb, age, span = here
+    return (
+        here,
+        (1 - turb, age, span),
+        (turb, age - 1, span),
+        (turb, age + 1, span),
+        (turb, age, lax.rem(span + spans - 1, spans)),
+        (turb, age, lax.rem(span + 1, spans)),
+    )
+
+
+def greet(ages_count):
+    here, other, below, above, prior, following = place()
+    barrier = pltpu.get_barrier_semaphore()
+    for device in (other, prior, following):
+        pl.semaphore_signal(barrier, inc=1, device_id=device, device_id_type=MESH)
+
+    @pl.when(here[1] > 0)
+    def _():
+        pl.semaphore_signal(barrier, inc=1, device_id=below, device_id_type=MESH)
+
+    @pl.when(here[1] < ages_count - 1)
+    def _():
+        pl.semaphore_signal(barrier, inc=1, device_id=above, device_id_type=MESH)
+
+    inner = (here[1] > 0).astype(jnp.int32) + (here[1] < ages_count - 1).astype(jnp.int32)
+    pl.semaphore_wait(barrier, 3 + inner)
+
+
+def keeps(stations, ages, shape):
+    lane = lax.broadcasted_iota(jnp.int32, shape, 1)
+    row = lax.broadcasted_iota(jnp.int32, shape, 0)
+    last_age = lax.axis_index("age") == lax.axis_size("age") - 1
+    last_station = lax.axis_index("span") == lax.axis_size("span") - 1
+    trail = jnp.where(jnp.logical_and(last_age, lane == ages - 1), 0.0, 1.0)
+    shed = jnp.where(jnp.logical_and(last_station, row % stations == stations - 1), 0.0, 1.0)
+    return trail, shed
+
+
+def gather_all(
+    blocks, stations, per_owner, positions_ref, strengths_ref, core_ref, seed_ref, table_ref,
+    strengths_buf, halo_buf, seed_buf, load_sems, halo_sems, send_sems, recv_sems,
 ):
+    ages = table_ref.shape[-1]
+    count = lax.axis_size("age")
+    halo = blocks // stations
+    here, other, below, above, prior, following = place()
+    turb, age, span = here
+    me = turb * count + age
+    mate = (1 - turb) * count + age
+    extra = per_owner - 6 * blocks
+    parts = (
+        (0, 3 * blocks),
+        (3 * blocks, 2 * blocks),
+        (5 * blocks, per_owner - 5 * blocks),
+    )
+    base = me * per_owner
+    loads = [
+        pltpu.make_async_copy(source, target, load_sems.at[k])
+        for k, (source, target) in enumerate(
+            (
+                (positions_ref, table_ref.at[pl.ds(pl.multiple_of(base, 8), 3 * blocks)]),
+                (strengths_ref, strengths_buf),
+                (core_ref, table_ref.at[pl.ds(pl.multiple_of(base + 5 * blocks, 8), blocks)]),
+                (seed_ref, seed_buf),
+            )
+        )
+    ]
+    for load in loads:
+        load.start()
+    halo_buf[...] = jnp.zeros_like(halo_buf)
+    trail, shed = keeps(stations, ages, (blocks, ages))
+    greet(count)
+
+    def rows(owner, part):
+        return pl.ds(pl.multiple_of(owner * per_owner + parts[part][0], 8), parts[part][1])
+
+    def copy(owner, part, way):
+        at = rows(owner, part)
+        return pltpu.make_async_remote_copy(
+            src_ref=table_ref.at[at],
+            dst_ref=table_ref.at[at],
+            send_sem=send_sems.at[way, part, owner],
+            recv_sem=recv_sems.at[part, owner],
+            device_id=(other, below, above)[way],
+            device_id_type=MESH,
+        )
+
+    def arrive(owner, part):
+        copy(owner, part, 0).wait_recv()
+
+    has_below = age > 0
+    has_above = age < count - 1
+
+    def share(owner, part):
+        @pl.when(has_below)
+        def _():
+            copy(owner, part, 1).start()
+
+        @pl.when(has_above)
+        def _():
+            copy(owner, part, 2).start()
+
+    loads[0].wait()
+    share(me, 0)
+    copy(me, 0, 0).start()
+    for k in range(3 * halo):
+        halo_buf[pl.ds(k, 1), :] = table_ref[pl.ds(base + k * stations, 1), :]
+    halo_copy = pltpu.make_async_remote_copy(
+        src_ref=halo_buf,
+        dst_ref=table_ref.at[pl.ds(pl.multiple_of(base + 6 * blocks, 8), extra)],
+        send_sem=halo_sems.at[0],
+        recv_sem=halo_sems.at[1],
+        device_id=prior,
+        device_id_type=MESH,
+    )
+    halo_copy.start()
+    loads[1].wait()
+    table_ref[pl.ds(pl.multiple_of(base + 3 * blocks, 8), blocks), :] = (
+        strengths_buf[pl.ds(0, blocks), :] * trail
+    )
+    table_ref[pl.ds(pl.multiple_of(base + 4 * blocks, 8), blocks), :] = (
+        strengths_buf[pl.ds(blocks, blocks), :] * shed
+    )
+    share(me, 1)
+    copy(me, 1, 0).start()
+    loads[2].wait()
+    loads[3].wait()
+    halo_copy.wait_recv()
+    copy(me, 2, 0).start()
+    share(me, 2)
+    arrive(mate, 2)
+    share(mate, 2)
+    for step in range(1, count):
+        for part in range(3):
+            for way, sign in ((2, -1), (1, 1)):
+                source = age + sign * step
+                onward = has_above if way == 2 else has_below
+
+                @pl.when(source >= 0 if sign < 0 else source < count)
+                def _(source=source, way=way, onward=onward, part=part):
+                    for column in (turb, 1 - turb)[: 2 if part == 2 else 1]:
+                        owner = column * count + source
+                        arrive(owner, part)
+
+                        @pl.when(onward)
+                        def _(owner=owner):
+                            copy(owner, part, way).start()
+
+                        if part < 2:
+                            copy(owner, part, 0).start()
+
+    for source in range(count):
+        for part in range(2):
+            arrive((1 - turb) * count + source, part)
+    halo_copy.wait_send()
+    copy(me, 2, 0).wait_send()
+    for source in range(count):
+        sent = [(turb * count + source, part) for part in range(3)]
+        sent.append(((1 - turb) * count + source, 2))
+        for part in range(2):
+            copy(sent[part][0], part, 0).wait_send()
+
+        @pl.when(jnp.logical_and(source >= age, has_below))
+        def _(sent=sent):
+            for owner, part in sent:
+                copy(owner, part, 1).wait_send()
+
+        @pl.when(jnp.logical_and(source <= age, has_above))
+        def _(sent=sent):
+            for owner, part in sent:
+                copy(owner, part, 2).wait_send()
+
+
+def exact_dot(selector, terms):
+    parts = [jnp.dot(selector, term, preferred_element_type=jnp.float32) for term in terms]
+    return (parts[2] + parts[1]) + parts[0]
+
+
+def split_terms(value):
+    high = value.astype(jnp.bfloat16)
+    rest = value - high.astype(jnp.float32)
+    middle = rest.astype(jnp.bfloat16)
+    low = (rest - middle.astype(jnp.float32)).astype(jnp.bfloat16)
+    return high, middle, low
+
+
+def step_kernel(
+    blocks, stations, per_owner, grad_rows, early, target_ref, owner_ref, source_ref,
+    target_row, owner_row, source_row, positions_ref, strengths_ref, core_ref, seed_ref,
+    advected_ref, positions_grad_ref, strengths_grad_ref,
+    table_ref, strengths_buf, halo_buf, seed_buf, rows_buf, values, terms, grads_ref, base_ref,
+    work, from_mate, from_below, from_above, late_in, halo_out, halo_in,
+    load_sems, start_sems, send_sems, recv_sems,
+    mate_sems, chain_send, chain_recv, late_sems, halo_sems,
+):
+    ages = grads_ref.shape[-1]
+    count = lax.axis_size("age")
+    halo = blocks // stations
+    here, other, below, above, prior, following = place()
+    turb, age, span = here
+    late = grad_rows - early
+    half = (early + 2 * late) // 16 * 8
+    cut = half - 2 * late
+    pieces = ((0, cut), (cut, early - cut))
+    group = 2 * count
     pairs = target_ref.shape[0]
-    me = lax.axis_index("turb") * lax.axis_size("age") + lax.axis_index("age")
+    me = turb * count + age
     own_rows = me * per_owner
-    ages = table_ref.shape[-1]
-    halo = blocks // stations
-    acc[...] = jnp.zeros_like(acc)
-    tgt_acc[...] = jnp.zeros_like(tgt_acc)
+
+    gather_all(
+        blocks, stations, per_owner, positions_ref, strengths_ref, core_ref, seed_ref, table_ref,
+        strengths_buf, halo_buf, seed_buf, load_sems, start_sems, send_sems, recv_sems,
+    )
 
     def tile(t, _):
         for j in range(TILE):
@@ -338,261 +551,60 @@
                 rows_buf[pl.ds((6 + r) * TILE + j, 1), :] = table_ref[pl.ds(nxt + r * blocks, 1), :]
                 rows_buf[pl.ds((9 + r) * TILE + j, 1), :] = table_ref[pl.ds(shed + r * shed_step, 1), :]
                 rows_buf[pl.ds((12 + r) * TILE + j, 1), :] = table_ref[pl.ds(own + r * blocks, 1), :]
-                rows_buf[pl.ds((15 + r) * TILE + j, 1), :] = seed_ref[pl.ds(tgt + r * blocks, 1), :] * time_step
+                rows_buf[pl.ds((15 + r) * TILE + j, 1), :] = (
+                    seed_buf[pl.ds(tgt + r * blocks, 1), :] * time_step
+                )
         rows = [rows_buf[pl.ds(r * TILE, TILE), :] for r in range(18)]
-        grad_source, out = pair_tile(rows, ages)
-        for r in range(11):
-            src_buf[pl.ds(t * (TILE * SRC_ROWS) + r, TILE, stride=SRC_ROWS), :] = grad_source[r]
-        for r in range(6):
-            tgt_buf[pl.ds(t * (TILE * TGT_ROWS) + r, TILE, stride=TGT_ROWS), :] = out[r]
+        for r, value in enumerate(pair_tile(rows, ages)):
+            values[pl.ds(pl.multiple_of(t * TILE, TILE), TILE), pl.ds(r * ages, ages)] = value
         return 0
 
     lax.fori_loop(0, pairs // TILE, tile, 0)
-
-    def scatter(p, _):
-        at = pl.ds(
-            pl.multiple_of((owner_ref[p] * blocks + source_ref[p] + 1) * SRC_ROWS, SRC_ROWS), SRC_ROWS
+    for k, term in enumerate(split_terms(values[...])):
+        terms[k] = term
+
+    def select(rows, chosen, which):
+        row = lax.broadcasted_iota(jnp.int32, (rows, pairs), 0)
+        hit = jnp.logical_and(row == chosen, which)
+        return jnp.where(hit, 1.0, 0.0).astype(jnp.bfloat16)
+
+    def columns(first, number):
+        return [terms[k, :, pl.ds(first * ages, number * ages)] for k in range(3)]
+
+    owners = owner_row[...]
+    sources = source_row[...]
+    followers = jnp.where(owners == group - 1, 0, owners + 1)
+    inner_row = sources % stations < stations - 1
+    lane_first = lax.broadcasted_iota(jnp.int32, (blocks, ages), 1) == 0
+    extra = grad_rows - 5 * blocks
+
+    def scatter(column, dest):
+        owner = column * count + dest
+        from_here = owners == owner
+        main = exact_dot(select(blocks, sources, from_here), columns(0, 5))
+        inner_shed = exact_dot(
+            select(blocks, sources + 1, jnp.logical_and(from_here, inner_row)), columns(5, 3)
         )
-        acc[at, :] += src_buf[pl.ds(pl.multiple_of(p * SRC_ROWS, SRC_ROWS), SRC_ROWS), :]
-        at = pl.ds(pl.multiple_of(target_ref[p] * TGT_ROWS, TGT_ROWS), TGT_ROWS)
-        tgt_acc[at, :] += tgt_buf[pl.ds(pl.multiple_of(p * TGT_ROWS, TGT_ROWS), TGT_ROWS), :]
-        return 0
-
-    lax.fori_loop(0, pairs, scatter, 0, unroll=8)
-
-    for c in range(3):
-        for q in range(0, blocks, 8):
-            at = pl.ds(c * blocks + q, 8)
-            velocity = tgt_acc[pl.ds(q * TGT_ROWS + c, 8, stride=TGT_ROWS), :]
-            here = table_ref[pl.ds(pl.multiple_of(own_rows + c * blocks + q, 8), 8), :]
-            advected_ref[at, :] = here + time_step * (velocity + 1.0 if c == 0 else velocity)
-            base_ref[at, :] = seed_ref[at, :] + tgt_acc[pl.ds(q * TGT_ROWS + 3 + c, 8, stride=TGT_ROWS), :]
-
-    lane = lax.broadcasted_iota(jnp.int32, (TILE, ages), 1)
-    sub = lax.broadcasted_iota(jnp.int32, (TILE, ages), 0)
-
-    def fold(o, _):
-        prev = lax.rem(o + group - 1, group)
-
-        def rows_of(owner, q, r):
-            return acc[pl.ds((owner * blocks + q + 1) * SRC_ROWS + r, 8, stride=SRC_ROWS), :]
-
-        base = o * grad_rows
-        for q in range(0, blocks, 8):
-            for c in range(3):
-                trail = jnp.where(lane == ages - 1, rows_of(prev, q, 3 + c), rows_of(o, q, 3 + c))
-                shed = rows_of(o, q - 1, 6 + c)
-                if q % stations == 0:
-                    shed = jnp.where(sub == 0, 0.0, shed)
-                grad_ref[pl.ds(base + c * blocks + q, 8), :] = (
-                    rows_of(o, q, c) + pltpu.roll(trail, 1, 1) + shed
-                )
-            for c in range(2):
-                grad_ref[pl.ds(base + (3 + c) * blocks + q, 8), :] = rows_of(o, q, 9 + c)
-        for c in range(3):
-            for h in range(halo):
-                row = (o * blocks + h * stations + stations) * SRC_ROWS + 6 + c
-                grad_ref[pl.ds(base + 5 * blocks + c * halo + h, 1), :] = acc[pl.ds(row, 1), :]
-        grad_ref[pl.ds(base + 5 * blocks + 3 * halo, grad_rows - 5 * blocks - 3 * halo), :] = (
-            jnp.zeros((grad_rows - 5 * blocks - 3 * halo, ages), jnp.float32)
+        outer_shed = exact_dot(
+            select(
+                -(-halo // 8) * 8,
+                sources // stations,
+                jnp.logical_and(from_here, jnp.logical_not(inner_row)),
+            ),
+            columns(5, 3),
         )
-        return 0
-
-    lax.fori_loop(0, group, fold, 0)
-
-
-MESH = pl.DeviceIdType.MESH
-
-
-def place():
-    here = (lax.axis_index("turb"), lax.axis_index("age"), lax.axis_index("span"))
-    spans = lax.axis_size("span")
-    turb, age, span = here
-    return (
-        here,
-        (1 - turb, age, span),
-        (turb, age - 1, span),
-        (turb, age + 1, span),
-        (turb, age, lax.rem(span + spans - 1, spans)),
-        (turb, age, lax.rem(span + 1, spans)),
-    )
-
-
-def greet(ages_count):
-    here, other, below, above, prior, following = place()
-    barrier = pltpu.get_barrier_semaphore()
-    for device in (other, prior, following):
-        pl.semaphore_signal(barrier, inc=1, device_id=device, device_id_type=MESH)
-
-    @pl.when(here[1] > 0)
-    def _():
-        pl.semaphore_signal(barrier, inc=1, device_id=below, device_id_type=MESH)
-
-    @pl.when(here[1] < ages_count - 1)
-    def _():
-        pl.semaphore_signal(barrier, inc=1, device_id=above, device_id_type=MESH)
-
-    inner = (here[1] > 0).astype(jnp.int32) + (here[1] < ages_count - 1).astype(jnp.int32)
-    pl.semaphore_wait(barrier, 3 + inner)
-
-
-def keeps(stations, ages, shape):
-    lane = lax.broadcasted_iota(jnp.int32, shape, 1)
-    row = lax.broadcasted_iota(jnp.int32, shape, 0)
-    last_age = lax.axis_index("age") == lax.axis_size("age") - 1
-    last_station = lax.axis_index("span") == lax.axis_size("span") - 1
-    trail = jnp.where(jnp.logical_and(last_age, lane == ages - 1), 0.0, 1.0)
-    shed = jnp.where(jnp.logical_and(last_station, row % stations == stations - 1), 0.0, 1.0)
-    return trail, shed
-
-
-def gather_kernel(
-    blocks, stations, per_owner, positions_ref, strengths_ref, core_ref, table_ref,
-    strengths_buf, halo_buf, load_sems, halo_sems, send_sems, recv_sems,
-):
-    ages = table_ref.shape[-1]
-    count = lax.axis_size("age")
-    halo = blocks // stations
-    here, other, below, above, prior, following = place()
-    turb, age, span = here
-    me = turb * count + age
-    mate = (1 - turb) * count + age
-    extra = per_owner - 6 * blocks
-    parts = (
-        (0, 3 * blocks),
-        (3 * blocks, 2 * blocks),
-        (5 * blocks, per_owner - 5 * blocks),
-    )
-    base = me * per_owner
-    loads = [
-        pltpu.make_async_copy(source, target, load_sems.at[k])
-        for k, (source, target) in enumerate(
-            (
-                (positions_ref, table_ref.at[pl.ds(pl.multiple_of(base, 8), 3 * blocks)]),
-                (strengths_ref, strengths_buf),
-                (core_ref, table_ref.at[pl.ds(pl.multiple_of(base + 5 * blocks, 8), blocks)]),
-            )
-        )
-    ]
-    for load in loads:
-        load.start()
-    halo_buf[...] = jnp.zeros_like(halo_buf)
-    trail, shed = keeps(stations, ages, (blocks, ages))
-    greet(count)
-
-    def rows(owner, part):
-        return pl.ds(pl.multiple_of(owner * per_owner + parts[part][0], 8), parts[part][1])
-
-    def copy(owner, part, way):
-        at = rows(owner, part)
-        return pltpu.make_async_remote_copy(
-            src_ref=table_ref.at[at],
-            dst_ref=table_ref.at[at],
-            send_sem=send_sems.at[way, part, owner],
-            recv_sem=recv_sems.at[part, owner],
-            device_id=(other, below, above)[way],
-            device_id_type=MESH,
-        )
-
-    def arrive(owner, part):
-        copy(owner, part, 0).wait_recv()
-
-    has_below = age > 0
-    has_above = age < count - 1
-
-    def share(owner, part):
-        @pl.when(has_below)
-        def _():
-            copy(owner, part, 1).start()
-
-        @pl.when(has_above)
-        def _():
-            copy(owner, part, 2).start()
-
-    loads[0].wait()
-    share(me, 0)
-    copy(me, 0, 0).start()
-    for k in range(3 * halo):
-        halo_buf[pl.ds(k, 1), :] = table_ref[pl.ds(base + k * stations, 1), :]
-    halo_copy = pltpu.make_async_remote_copy(
-        src_ref=halo_buf,
-        dst_ref=table_ref.at[pl.ds(pl.multiple_of(base + 6 * blocks, 8), extra)],
-        send_sem=halo_sems.at[0],
-        recv_sem=halo_sems.at[1],
-        device_id=prior,
-        device_id_type=MESH,
-    )
-    halo_copy.start()
-    loads[1].wait()
-    table_ref[pl.ds(pl.multiple_of(base + 3 * blocks, 8), blocks), :] = (
-        strengths_buf[pl.ds(0, blocks), :] * trail
-    )
-    table_ref[pl.ds(pl.multiple_of(base + 4 * blocks, 8), blocks), :] = (
-        strengths_buf[pl.ds(blocks, blocks), :] * shed
-    )
-    share(me, 1)
-    copy(me, 1, 0).start()
-    loads[2].wait()
-    halo_copy.wait_recv()
-    copy(me, 2, 0).start()
-    share(me, 2)
-    arrive(mate, 2)
-    share(mate, 2)
-    for step in range(1, count):
-        for part in range(3):
-            for way, sign in ((2, -1), (1, 1)):
-                source = age + sign * step
-                onward = has_above if way == 2 else has_below
-
-                @pl.when(source >= 0 if sign < 0 else source < count)
-                def _(source=source, way=way, onward=onward, part=part):
-                    for column in (turb, 1 - turb)[: 2 if part == 2 else 1]:
-                        owner = column * count + source
-                        arrive(owner, part)
-
-                        @pl.when(onward)
-                        def _(owner=owner):
-                            copy(owner, part, way).start()
-
-                        if part < 2:
-                            copy(owner, part, 0).start()
-
-    for source in range(count):
-        for part in range(2):
-            arrive((1 - turb) * count + source, part)
-    halo_copy.wait_send()
-    copy(me, 2, 0).wait_send()
-    for source in range(count):
-        sent = [(turb * count + source, part) for part in range(3)]
-        sent.append(((1 - turb) * count + source, 2))
-        for part in range(2):
-            copy(sent[part][0], part, 0).wait_send()
-
-        @pl.when(jnp.logical_and(source >= age, has_below))
-        def _(sent=sent):
-            for owner, part in sent:
-                copy(owner, part, 1).wait_send()
-
-        @pl.when(jnp.logical_and(source <= age, has_above))
-        def _(sent=sent):
-            for owner, part in sent:
-                copy(owner, part, 2).wait_send()
-
-
-def reduce_kernel(
-    blocks, stations, grad_rows, early, grads_ref, base_ref, positions_grad_ref, strengths_grad_ref,
-    work, from_mate, from_below, from_above, late_in, halo_out, halo_in,
-    mate_sems, chain_send, chain_recv, late_sems, halo_sems,
-):
-    ages = grads_ref.shape[-1]
-    count = lax.axis_size("age")
-    halo = blocks // stations
-    here, other, below, above, prior, following = place()
-    turb, age, span = here
-    late = grad_rows - early
-    half = (early + 2 * late) // 16 * 8
-    cut = half - 2 * late
-    pieces = ((0, cut), (cut, early - cut))
+        carry = exact_dot(select(blocks, sources, followers == owner), columns(8, 1))
+        for r in range(5):
+            value = main[:, r * ages : (r + 1) * ages]
+            if r < 3:
+                lane0 = pltpu.roll(carry, ages - r, 1) if r else carry
+                value = value + inner_shed[:, r * ages : (r + 1) * ages]
+                value = value + jnp.where(lane_first, lane0, 0.0)
+            grads_ref[part(column, dest, r * blocks, blocks), :] = value
+        outer = [outer_shed[0:halo, r * ages : (r + 1) * ages] for r in range(3)]
+        if extra > 3 * halo:
+            outer.append(jnp.zeros((extra - 3 * halo, ages), jnp.float32))
+        grads_ref[part(column, dest, 5 * blocks, extra), :] = jnp.concatenate(outer)
     spans = ((0, half), (half, early + 2 * late - half))
     has_below = age > 0
     has_above = age < count - 1
@@ -634,12 +646,16 @@
             rank = rank + valid.astype(jnp.int32)
     steps = [(order[k], piece) for k in range(count) for piece in range(2)]
 
-    greet(count)
+    scatter(1 - turb, order[0])
     mate_copy(*steps[0]).start()
     mate_copy(*steps[1]).start()
 
     def take(number):
         dest, piece = steps[number]
+        if piece == 0:
+            scatter(turb, dest)
+            if number + 2 < len(steps):
+                scatter(1 - turb, steps[number + 2][0])
         mate_copy(dest, piece).wait_recv()
         if number + 2 < len(steps):
             mate_copy(*steps[number + 2]).start()
@@ -665,7 +681,15 @@
         pl.when(dest > age)(lambda: chain_copy(dest, piece, True).start())
         pl.when(dest < age)(lambda: chain_copy(dest, piece, False).start())
 
-    for number in range(len(steps) - 1):
+    take(0)
+    target_sums = exact_dot(select(blocks, target_row[...], target_row[...] >= 0), columns(9, 6))
+    for c in range(3):
+        at = pl.ds(c * blocks, blocks)
+        velocity = target_sums[:, c * ages : (c + 1) * ages]
+        here_rows = table_ref[pl.ds(pl.multiple_of(own_rows + c * blocks, 8), blocks), :]
+        advected_ref[at, :] = here_rows + time_step * (velocity + 1.0 if c == 0 else velocity)
+        base_ref[at, :] = seed_buf[at, :] + target_sums[:, (3 + c) * ages : (4 + c) * ages]
+    for number in range(1, len(steps) - 1):
         take(number)
     late_copy = pltpu.make_async_remote_copy(
         src_ref=work.at[age, pl.ds(late, late)],
@@ -726,68 +750,43 @@
     grad_rows = -(-(5 * blocks + 3 * halo) // 8) * 8
     early = grad_rows * 5 // 6 // 8 * 8
     late = grad_rows - early
+    extra = grad_rows - 5 * blocks
     vmem = pl.BlockSpec(memory_space=pltpu.VMEM)
-    limit = 40 * 1024 * 1024
+    smem = pl.BlockSpec(memory_space=pltpu.SMEM)
+    kept = pl.BlockSpec(memory_space=pl.ANY)
     dma = pltpu.SemaphoreType.DMA
-    rows = positions.reshape(3 * blocks, ages)
-    table = pl.pallas_call(
-        functools.partial(gather_kernel, blocks, stations, per_owner),
-        out_shape=jax.ShapeDtypeStruct((group * per_owner, ages), jnp.float32),
-        in_specs=[pl.BlockSpec(memory_space=pl.ANY)] * 3,
-        out_specs=vmem,
+    rows_out = jax.ShapeDtypeStruct((3 * blocks, ages), jnp.float32)
+
+    def room(*shape):
+        return pltpu.VMEM(shape + (ages,), jnp.float32)
+
+    lists = (pair_target, pair_owner, pair_source)
+    advected, grad_positions, grad_strengths = pl.pallas_call(
+        functools.partial(step_kernel, blocks, stations, per_owner, grad_rows, early),
+        out_shape=(rows_out, rows_out, jax.ShapeDtypeStruct((2 * blocks, ages), jnp.float32)),
+        in_specs=[smem] * 3 + [vmem] * 3 + [kept] * 4,
+        out_specs=(vmem, vmem, vmem),
         scratch_shapes=[
-            pltpu.VMEM((2 * blocks, ages), jnp.float32),
-            pltpu.VMEM((per_owner - 6 * blocks, ages), jnp.float32),
-            dma((3,)),
+            room(group * per_owner),
+            room(2 * blocks),
+            room(per_owner - 6 * blocks),
+            room(3 * blocks),
+            room(18 * TILE),
+            pltpu.VMEM((pairs, 15 * ages), jnp.float32),
+            pltpu.VMEM((3, pairs, 15 * ages), jnp.bfloat16),
+            room(group * grad_rows),
+            room(3 * blocks),
+            room(count, early + 2 * late),
+            room(count, early),
+            room(count, early + 2 * late),
+            room(count, early + 2 * late),
+            room(late),
+            room(extra),
+            room(extra),
+            dma((4,)),
             dma((2,)),
             dma((3, 3, group)),
             dma((3, group)),
-        ],
-        compiler_params=pltpu.CompilerParams(
-            collective_id=0, has_side_effects=True, vmem_limit_bytes=limit
-        ),
-    )(rows, strengths.reshape(2 * blocks, ages), core_radius.reshape(blocks, ages))
-    seeds = adjoint_seed.reshape(3 * blocks, ages)
-    smem = pl.BlockSpec(memory_space=pltpu.SMEM)
-    rows_out = jax.ShapeDtypeStruct((3 * blocks, ages), jnp.float32)
-    grads, advected, grad_base = pl.pallas_call(
-        functools.partial(pairs_kernel, group, blocks, stations, per_owner, grad_rows),
-        out_shape=(
-            jax.ShapeDtypeStruct((group * grad_rows, ages), jnp.float32),
-            rows_out,
-            rows_out,
-        ),
-        in_specs=[smem, smem, smem, vmem, vmem],
-        out_specs=(vmem, vmem, vmem),
-        scratch_shapes=[
-            pltpu.VMEM((18 * TILE, ages), jnp.float32),
-            pltpu.VMEM((pairs * SRC_ROWS, ages), jnp.float32),
-            pltpu.VMEM((pairs * TGT_ROWS, ages), jnp.float32),
-            pltpu.VMEM(((group * blocks + 1) * SRC_ROWS, ages), jnp.float32),
-            pltpu.VMEM((blocks * TGT_ROWS, ages), jnp.float32),
-        ],
-        compiler_params=pltpu.CompilerParams(vmem_limit_bytes=limit),
-    )(
-        pair_target.reshape(pairs),
-        pair_owner.reshape(pairs),
-        pair_source.reshape(pairs),
-        table,
-        seeds,
-    )
-    extra = grad_rows - 5 * blocks
-    grad_positions, grad_strengths = pl.pallas_call(
-        functools.partial(reduce_kernel, blocks, stations, grad_rows, early),
-        out_shape=(rows_out, jax.ShapeDtypeStruct((2 * blocks, ages), jnp.float32)),
-        in_specs=[vmem] * 2,
-        out_specs=(vmem, vmem),
-        scratch_shapes=[
-            pltpu.VMEM((count, early + 2 * late, ages), jnp.float32),
-            pltpu.VMEM((count, early, ages), jnp.float32),
-            pltpu.VMEM((count, early + 2 * late, ages), jnp.float32),
-            pltpu.VMEM((count, early + 2 * late, ages), jnp.float32),
-            pltpu.VMEM((late, ages), jnp.float32),
-            pltpu.VMEM((extra, ages), jnp.float32),
-            pltpu.VMEM((extra, ages), jnp.float32),
             dma((2, count, 2)),
             dma((count, 2)),
             dma((2, count, 2)),
@@ -795,9 +794,16 @@
             dma((2,)),
         ],
         compiler_params=pltpu.CompilerParams(
-            collective_id=1, has_side_effects=True, vmem_limit_bytes=limit
+            collective_id=0, has_side_effects=True, vmem_limit_bytes=60 * 1024 * 1024
         ),
-    )(grads, grad_base)
+    )(
+        *[pair.reshape(pairs) for pair in lists],
+        *[pair.reshape(1, pairs) for pair in lists],
+        positions.reshape(3 * blocks, ages),
+        strengths.reshape(2 * blocks, ages),
+        core_radius.reshape(blocks, ages),
+        adjoint_seed.reshape(3 * blocks, ages),
+    )
     return (
         advected.reshape(shape_here),
         grad_positions.reshape(shape_here),

time: 85.4 us -> 80.1 us (0.938)
  Pallas kernels: 80.5 us -> 76.1 us
    pallas_call x3 -> x1, Pallas kernels: 80.5 us -> 76.1 us  [local_dense(): pl.pallas_call(functools.partial(step_kernel, blocks, stations, per_owner...]
    unnamed x16 -> x7, local copies, waits for them, and re-layouts: 3.93 us -> 3.21 us
where the time goes in v5:
time: 80.1 us; the launch traced here: 79.9 us
  Pallas kernels  76.1 us (95%)
  local copies, waits for them, and re-layouts  3.21 us (4%)
    pallas_call x1, Pallas kernels, local_dense(): pl.pallas_call(functools.partial(step_kernel, blocks, stations, per_owner...  76.1 us
    unnamed x7, local copies, waits for them, and re-layouts  3.21 us

profile of v5, /device:TPU:0, one launch (start us, length us, event | category | flops | bytes accessed | tf_op | source)
XLA Modules:
  0.0 79.9 jit_solution(13003578582775309300)
XLA Ops:
  0.6 76.1 %shard_map.94 = (f32[288,128]{1,0:T(8,128)}, f32[288,128]{1,0:T(8,128)}, f32[192,128]{1,0:T(8,128)}) custom-call(s32[128]{0:T(128)} %bitcast.20, s32[128]{0:T(128)} %bitcast.22, s32[128]{0:T(128)} %bitcast.24, s32[1,128]{1,0:T(1,128)} %bitcast.21, s32[1,128]{1,0:T(1,128)} %bitcast.23, s32[1,128]{1,0:T(1,128)} %bitcast.25, f32[288,128]{1,0:T(8,128)} %bitcast.13, ...), custom_call_target="tpu_custom_call" | custom-call | tf_op jit(solution)/shard_map/pallas_call | solution.py:764
  76.7 0.0 copy-start
  76.7 1.6 %copy.13 = f32[3,2,3,16,128]{4,3,2,1,0:T(8,128)} copy(f32[3,2,3,16,128]{4,3,2,1,0:T(8,128)} %bitcast.16) | data formatting | bytes 294912
  78.4 0.0 copy-done
  78.4 0.0 copy-start.1
  78.4 0.7 copy.14
  79.0 0.3 copy-done.1
  79.3 0.6 copy.15
Async XLA Ops:
  76.7 1.6 %copy-start = (f32[288,128]{1,0:T(8,128)S(1)}, f32[288,128]{1,0:T(8,128)}, u32[]{:S(2)}) copy-start(f32[288,128]{1,0:T(8,128)} %get-tuple-element.7) | copy-start | bytes 442372
  78.4 0.9 %copy-start.1 = (f32[192,128]{1,0:T(8,128)S(1)}, f32[192,128]{1,0:T(8,128)}, u32[]{:S(2)}) copy-start(f32[192,128]{1,0:T(8,128)} %get-tuple-element.8) | copy-start | bytes 294916

commit v6 on v5

--- a/solution.py
+++ b/solution.py
@@ -220,11 +220,11 @@
     return a[0] * b[0] + a[1] * b[1] + a[2] * b[2]
 
 
-def segment(r0, r1, r2, inv1, cube1, gamma, core_sq, quad, quart, inside, w):
+def segment(r0, r1, r2, inv1, along_sq, gamma, core_sq, quad, quart, inside, w):
     c = cross(r0, r1)
     c_sq = dot(c, c)
     a = dot(r0, r1)
-    b = dot(r0, r2)
+    b = a - along_sq
     inv2 = lax.rsqrt(dot(r2, r2) + core_sq)
     proj = a * inv1 - b * inv2
     inv_d = lax.rsqrt(c_sq * c_sq + quart)
@@ -233,20 +233,19 @@
     m = gamma * inv_d
     k = m * proj
     gp = m * q
-    fd = (k * q) * (inv_d * inv_d)
+    fd = (k * q) * (2.0 * (inv_d * inv_d))
     grad_gamma = proj * (q * inv_d)
-    h = 2.0 * fd * c_sq
+    h = fd * c_sq
     gn2 = gp * b * (inv2 * inv2 * inv2)
     alpha = gp * (inv1 - inv2) - gn2
-    beta = gn2 - gp * a * cube1
-    delta = 2.0 * (gp * inv2 - fd * quad) + gn2
+    delta = gp * (inv2 + inv2) - fd * quad + gn2
     gc = tuple(k * w[i] - h * c[i] for i in range(3))
     left = cross(gc, r0)
     right = cross(r1, gc)
-    grad_r1 = tuple(left[i] + alpha * r0[i] + beta * r1[i] for i in range(3))
-    grad_r0 = tuple(right[i] + alpha * r1[i] + delta * r0[i] for i in range(3))
+    grad_r1 = tuple(left[i] + alpha * r0[i] for i in range(3))
+    grad_r0 = tuple(right[i] + alpha * r1[i] for i in range(3))
     velocity = tuple(k * c[i] for i in range(3))
-    return velocity, grad_r1, grad_r0, grad_gamma
+    return velocity, grad_r1, grad_r0, grad_gamma, delta, gn2, gp * a
 
 
 def pair_tile(rows, ages):
@@ -265,13 +264,15 @@
     alongs = [[trail[i] - begin[i] for i in range(3)], [rows[9 + i] - begin[i] for i in range(3)]]
     gammas = [rows[3] * (1.0 / four_pi), rows[4] * (1.0 / four_pi)]
     core_quad = core_sq * core_sq
-    lengths = [dot(r0, r0) + core_sq for r0 in alongs]
+    alongs_sq = [dot(r0, r0) for r0 in alongs]
+    lengths = [along_sq + core_sq for along_sq in alongs_sq]
     quads = [core_quad * length for length in lengths]
     quarts = [quad * length for quad, length in zip(quads, lengths)]
     zero = jnp.zeros((TILE, ages), jnp.float32)
     sum_r1 = [zero] * 3
     sum_r0 = [[zero] * 3, [zero] * 3]
     sum_gamma = [zero, zero]
+    sum_delta = [zero, zero]
     out = [zero] * 6
     for offset in range(-REACH, REACH):
         shift = offset % ages
@@ -283,24 +284,31 @@
             inside = lane < ages + offset
         r1 = [target[i] - begin[i] for i in range(3)]
         inv1 = lax.rsqrt(dot(r1, r1) + core_sq)
-        cube1 = inv1 * inv1 * inv1
+        beta = [None, None]
+        ga = [None, None]
         vel = [None] * 3
         g1 = [None] * 3
         for kind in range(2):
             r0 = alongs[kind]
             r2 = [r1[i] - r0[i] for i in range(3)]
-            v, d1, d0, dg = segment(
-                r0, r1, r2, inv1, cube1, gammas[kind], core_sq,
+            v, d1, d0, dg, delta, beta[kind], ga[kind] = segment(
+                r0, r1, r2, inv1, alongs_sq[kind], gammas[kind], core_sq,
                 quads[kind], quarts[kind], inside, w,
             )
             vel = [v[i] if kind == 0 else vel[i] + v[i] for i in range(3)]
             g1 = [d1[i] if kind == 0 else g1[i] + d1[i] for i in range(3)]
             sum_r0[kind] = [sum_r0[kind][i] + d0[i] for i in range(3)]
             sum_gamma[kind] = sum_gamma[kind] + dg
+            sum_delta[kind] = sum_delta[kind] + delta
+        pull = (beta[0] + beta[1]) - (ga[0] + ga[1]) * (inv1 * inv1 * inv1)
+        g1 = [g1[i] + pull * r1[i] for i in range(3)]
         sum_r1 = [sum_r1[i] + g1[i] for i in range(3)]
         back = (-offset) % ages
         both = vel + g1
         out = [out[i] + (pltpu.roll(both[i], back, 1) if back else both[i]) for i in range(6)]
+    sum_r0 = [
+        [sum_r0[kind][i] + sum_delta[kind] * alongs[kind][i] for i in range(3)] for kind in range(2)
+    ]
     carry = zero
     grad_begin = []
     for i in range(3):
@@ -473,23 +481,26 @@
     for source in range(count):
         for part in range(2):
             arrive((1 - turb) * count + source, part)
-    halo_copy.wait_send()
-    copy(me, 2, 0).wait_send()
-    for source in range(count):
-        sent = [(turb * count + source, part) for part in range(3)]
-        sent.append(((1 - turb) * count + source, 2))
-        for part in range(2):
-            copy(sent[part][0], part, 0).wait_send()
-
-        @pl.when(jnp.logical_and(source >= age, has_below))
-        def _(sent=sent):
-            for owner, part in sent:
-                copy(owner, part, 1).wait_send()
-
-        @pl.when(jnp.logical_and(source <= age, has_above))
-        def _(sent=sent):
-            for owner, part in sent:
-                copy(owner, part, 2).wait_send()
+    def finish():
+        halo_copy.wait_send()
+        copy(me, 2, 0).wait_send()
+        for source in range(count):
+            sent = [(turb * count + source, part) for part in range(3)]
+            sent.append(((1 - turb) * count + source, 2))
+            for part in range(2):
+                copy(sent[part][0], part, 0).wait_send()
+
+            @pl.when(jnp.logical_and(source >= age, has_below))
+            def _(sent=sent):
+                for owner, part in sent:
+                    copy(owner, part, 1).wait_send()
+
+            @pl.when(jnp.logical_and(source <= age, has_above))
+            def _(sent=sent):
+                for owner, part in sent:
+                    copy(owner, part, 2).wait_send()
+
+    return finish
 
 
 def exact_dot(selector, terms):
@@ -508,7 +519,7 @@
 def step_kernel(
     blocks, stations, per_owner, grad_rows, early, target_ref, owner_ref, source_ref,
     target_row, owner_row, source_row, positions_ref, strengths_ref, core_ref, seed_ref,
-    advected_ref, positions_grad_ref, strengths_grad_ref,
+    moved_ref, positions_grad_ref, strengths_grad_ref,
     table_ref, strengths_buf, halo_buf, seed_buf, rows_buf, values, terms, grads_ref, base_ref,
     work, from_mate, from_below, from_above, late_in, halo_out, halo_in,
     load_sems, start_sems, send_sems, recv_sems,
@@ -528,12 +539,12 @@
     me = turb * count + age
     own_rows = me * per_owner
 
-    gather_all(
+    finish = gather_all(
         blocks, stations, per_owner, positions_ref, strengths_ref, core_ref, seed_ref, table_ref,
         strengths_buf, halo_buf, seed_buf, load_sems, start_sems, send_sems, recv_sems,
     )
 
-    def tile(t, _):
+    def fetch(t):
         for j in range(TILE):
             p = t * TILE + j
             tgt = target_ref[p]
@@ -551,14 +562,17 @@
                 rows_buf[pl.ds((6 + r) * TILE + j, 1), :] = table_ref[pl.ds(nxt + r * blocks, 1), :]
                 rows_buf[pl.ds((9 + r) * TILE + j, 1), :] = table_ref[pl.ds(shed + r * shed_step, 1), :]
                 rows_buf[pl.ds((12 + r) * TILE + j, 1), :] = table_ref[pl.ds(own + r * blocks, 1), :]
-                rows_buf[pl.ds((15 + r) * TILE + j, 1), :] = (
-                    seed_buf[pl.ds(tgt + r * blocks, 1), :] * time_step
-                )
+                rows_buf[pl.ds((15 + r) * TILE + j, 1), :] = seed_buf[pl.ds(tgt + r * blocks, 1), :]
+
+    def tile(t, _):
         rows = [rows_buf[pl.ds(r * TILE, TILE), :] for r in range(18)]
+        rows[15:18] = [seed * time_step for seed in rows[15:18]]
+        fetch(jnp.minimum(t + 1, pairs // TILE - 1))
         for r, value in enumerate(pair_tile(rows, ages)):
             values[pl.ds(pl.multiple_of(t * TILE, TILE), TILE), pl.ds(r * ages, ages)] = value
         return 0
 
+    fetch(0)
     lax.fori_loop(0, pairs // TILE, tile, 0)
     for k, term in enumerate(split_terms(values[...])):
         terms[k] = term
@@ -686,9 +700,8 @@
     for c in range(3):
         at = pl.ds(c * blocks, blocks)
         velocity = target_sums[:, c * ages : (c + 1) * ages]
-        here_rows = table_ref[pl.ds(pl.multiple_of(own_rows + c * blocks, 8), blocks), :]
-        advected_ref[at, :] = here_rows + time_step * (velocity + 1.0 if c == 0 else velocity)
-        base_ref[at, :] = seed_buf[at, :] + target_sums[:, (3 + c) * ages : (4 + c) * ages]
+        moved_ref[at, :] = time_step * (velocity + 1.0 if c == 0 else velocity)
+        base_ref[at, :] = target_sums[:, (3 + c) * ages : (4 + c) * ages]
     for number in range(1, len(steps) - 1):
         take(number)
     late_copy = pltpu.make_async_remote_copy(
@@ -728,6 +741,7 @@
     for k in range(3 * halo):
         at = pl.ds(k * stations, 1)
         positions_grad_ref[at, :] = positions_grad_ref[at, :] + halo_in[pl.ds(k, 1), :]
+    finish()
     late_copy.wait_send()
     halo_copy.wait_send()
     for dest in range(count):
@@ -761,7 +775,7 @@
         return pltpu.VMEM(shape + (ages,), jnp.float32)
 
     lists = (pair_target, pair_owner, pair_source)
-    advected, grad_positions, grad_strengths = pl.pallas_call(
+    moved, grad_moved, grad_strengths = pl.pallas_call(
         functools.partial(step_kernel, blocks, stations, per_owner, grad_rows, early),
         out_shape=(rows_out, rows_out, jax.ShapeDtypeStruct((2 * blocks, ages), jnp.float32)),
         in_specs=[smem] * 3 + [vmem] * 3 + [kept] * 4,
@@ -805,8 +819,8 @@
         adjoint_seed.reshape(3 * blocks, ages),
     )
     return (
-        advected.reshape(shape_here),
-        grad_positions.reshape(shape_here),
+        positions + moved.reshape(shape_here),
+        adjoint_seed + grad_moved.reshape(shape_here),
         grad_strengths.reshape(strengths.shape),
     )
 

time: 80.1 us -> 78.3 us (0.978)
  local copies, waits for them, and re-layouts: 3.21 us -> 0.89 us
  other arithmetic: 0 us -> 2.31 us
  Pallas kernels: 76.1 us -> 74.2 us
    unnamed x7 -> x9, local copies, waits for them, and re-layouts: 3.21 us -> 0.89 us
    add x0 -> x2, other arithmetic: none -> 2.31 us  [the longest x1 1.63 us: local_dense(): positions + moved.reshape(shape_here)]
    pallas_call x1, Pallas kernels: 76.1 us -> 74.2 us  [local_dense(): pl.pallas_call(functools.partial(step_kernel, blocks, stations, per_owner...]
where the time goes in v6:
time: 78.3 us; the launch traced here: 78.1 us
  Pallas kernels  74.2 us (95%)
  other arithmetic  2.31 us (3%)
  local copies, waits for them, and re-layouts  0.89 us (1%)
    pallas_call x1, Pallas kernels, local_dense(): pl.pallas_call(functools.partial(step_kernel, blocks, stations, per_owner...  74.2 us
    add x1, other arithmetic, local_dense(): positions + moved.reshape(shape_here)  1.63 us

profile of v6, /device:TPU:0, one launch (start us, length us, event | category | flops | bytes accessed | tf_op | source)
XLA Modules:
  0.0 78.1 jit_solution(8991686701852906483)
XLA Ops:
  0.6 0.0 copy-start
  0.6 74.2 %shard_map.94 = (f32[288,128]{1,0:T(8,128)}, f32[288,128]{1,0:T(8,128)}, f32[192,128]{1,0:T(8,128)}) custom-call(s32[128]{0:T(128)} %bitcast.20, s32[128]{0:T(128)} %bitcast.22, s32[128]{0:T(128)} %bitcast.24, s32[1,128]{1,0:T(1,128)} %bitcast.21, s32[1,128]{1,0:T(1,128)} %bitcast.23, s32[1,128]{1,0:T(1,128)} %bitcast.25, f32[288,128]{1,0:T(8,128)} %bitcast.13, ...), custom_call_target="tpu_custom_call" | custom-call | tf_op jit(solution)/shard_map/pallas_call | solution.py:778
  74.9 0.0 copy-done
  74.9 0.0 copy-start.1
  74.9 0.0 copy-start.2
  74.9 1.6 %add.6 = f32[3,2,3,16,128]{4,3,2,1,0:T(8,128)} add(f32[3,2,3,16,128]{4,3,2,1,0:T(8,128)S(1)} %copy-done, f32[3,2,3,16,128]{4,3,2,1,0:T(8,128)} %bitcast.16) | non-fusion elementwise | flops 36864 | bytes 442368 | tf_op jit(solution)/shard_map/add | solution.py:822
  76.5 0.0 copy-done.1
  76.5 0.0 copy-done.2
  76.5 0.0 copy-start.3
  76.5 0.7 add.7
  77.2 0.2 copy-done.3
  77.5 0.6 copy.11
Async XLA Ops:
  0.6 74.2 %copy-start = (f32[3,2,3,16,128]{4,3,2,1,0:T(8,128)S(1)}, f32[3,2,3,16,128]{4,3,2,1,0:T(8,128)}, u32[]{:S(2)}) copy-start(f32[3,2,3,16,128]{4,3,2,1,0:T(8,128)} %param.7) | copy-start | bytes 442372
  74.9 1.7 %copy-start.1 = (f32[3,2,3,16,128]{4,3,2,1,0:T(8,128)S(1)}, f32[3,2,3,16,128]{4,3,2,1,0:T(8,128)}, u32[]{:S(2)}) copy-start(f32[3,2,3,16,128]{4,3,2,1,0:T(8,128)} %param.10) | copy-start | bytes 442372
  74.9 1.6 %copy-start.2 = (f32[288,128]{1,0:T(8,128)S(1)}, f32[288,128]{1,0:T(8,128)}, u32[]{:S(2)}) copy-start(f32[288,128]{1,0:T(8,128)} %get-tuple-element.7) | copy-start | bytes 442372
  76.5 0.9 %copy-start.3 = (f32[192,128]{1,0:T(8,128)S(1)}, f32[192,128]{1,0:T(8,128)}, u32[]{:S(2)}) copy-start(f32[192,128]{1,0:T(8,128)} %get-tuple-element.8) | copy-start | bytes 294916

commit v7 on v6

--- a/solution.py
+++ b/solution.py
@@ -504,8 +504,9 @@
 
 
 def exact_dot(selector, terms):
-    parts = [jnp.dot(selector, term, preferred_element_type=jnp.float32) for term in terms]
-    return (parts[2] + parts[1]) + parts[0]
+    return jnp.dot(
+        jnp.concatenate([selector] * 3, axis=1), terms, preferred_element_type=jnp.float32
+    )
 
 
 def split_terms(value):
@@ -575,7 +576,7 @@
     fetch(0)
     lax.fori_loop(0, pairs // TILE, tile, 0)
     for k, term in enumerate(split_terms(values[...])):
-        terms[k] = term
+        terms[pl.ds(k * pairs, pairs), :] = term
 
     def select(rows, chosen, which):
         row = lax.broadcasted_iota(jnp.int32, (rows, pairs), 0)
@@ -583,7 +584,7 @@
         return jnp.where(hit, 1.0, 0.0).astype(jnp.bfloat16)
 
     def columns(first, number):
-        return [terms[k, :, pl.ds(first * ages, number * ages)] for k in range(3)]
+        return terms[:, pl.ds(first * ages, number * ages)]
 
     owners = owner_row[...]
     sources = source_row[...]
@@ -787,7 +788,7 @@
             room(3 * blocks),
             room(18 * TILE),
             pltpu.VMEM((pairs, 15 * ages), jnp.float32),
-            pltpu.VMEM((3, pairs, 15 * ages), jnp.bfloat16),
+            pltpu.VMEM((3 * pairs, 15 * ages), jnp.bfloat16),
             room(group * grad_rows),
             room(3 * blocks),
             room(count, early + 2 * late),

time: 78.3 us -> 78.2 us (level)
  no operation moved by 1% of the time
where the time goes in v7:
time: 78.2 us; the launch traced here: 78.1 us
  Pallas kernels  74.2 us (95%)
  other arithmetic  2.31 us (3%)
  local copies, waits for them, and re-layouts  0.89 us (1%)
    pallas_call x1, Pallas kernels, local_dense(): pl.pallas_call(functools.partial(step_kernel, blocks, stations, per_owner...  74.2 us
    add x1, other arithmetic, local_dense(): positions + moved.reshape(shape_here)  1.63 us

profile of v7, /device:TPU:0, one launch (start us, length us, event | category | flops | bytes accessed | tf_op | source)
XLA Modules:
  0.0 78.1 jit_solution(8454995156535497501)
XLA Ops:
  0.6 0.0 copy-start
  0.6 74.2 %shard_map.94 = (f32[288,128]{1,0:T(8,128)}, f32[288,128]{1,0:T(8,128)}, f32[192,128]{1,0:T(8,128)}) custom-call(s32[128]{0:T(128)} %bitcast.20, s32[128]{0:T(128)} %bitcast.22, s32[128]{0:T(128)} %bitcast.24, s32[1,128]{1,0:T(1,128)} %bitcast.21, s32[1,128]{1,0:T(1,128)} %bitcast.23, s32[1,128]{1,0:T(1,128)} %bitcast.25, f32[288,128]{1,0:T(8,128)} %bitcast.13, ...), custom_call_target="tpu_custom_call" | custom-call | tf_op jit(solution)/shard_map/pallas_call | solution.py:779
  74.8 0.0 copy-done
  74.8 0.0 copy-start.1
  74.9 0.0 copy-start.2
  74.9 1.6 %add.6 = f32[3,2,3,16,128]{4,3,2,1,0:T(8,128)} add(f32[3,2,3,16,128]{4,3,2,1,0:T(8,128)S(1)} %copy-done, f32[3,2,3,16,128]{4,3,2,1,0:T(8,128)} %bitcast.16) | non-fusion elementwise | flops 36864 | bytes 442368 | tf_op jit(solution)/shard_map/add | solution.py:823
  76.5 0.0 copy-done.1
  76.5 0.0 copy-done.2
  76.5 0.0 copy-start.3
  76.5 0.7 add.7
  77.2 0.2 copy-done.3
  77.4 0.6 copy.11
Async XLA Ops:
  0.6 74.2 %copy-start = (f32[3,2,3,16,128]{4,3,2,1,0:T(8,128)S(1)}, f32[3,2,3,16,128]{4,3,2,1,0:T(8,128)}, u32[]{:S(2)}) copy-start(f32[3,2,3,16,128]{4,3,2,1,0:T(8,128)} %param.7) | copy-start | bytes 442372
  74.8 1.7 %copy-start.1 = (f32[3,2,3,16,128]{4,3,2,1,0:T(8,128)S(1)}, f32[3,2,3,16,128]{4,3,2,1,0:T(8,128)}, u32[]{:S(2)}) copy-start(f32[3,2,3,16,128]{4,3,2,1,0:T(8,128)} %param.10) | copy-start | bytes 442372
  74.9 1.6 %copy-start.2 = (f32[288,128]{1,0:T(8,128)S(1)}, f32[288,128]{1,0:T(8,128)}, u32[]{:S(2)}) copy-start(f32[288,128]{1,0:T(8,128)} %get-tuple-element.7) | copy-start | bytes 442372
  76.5 0.9 %copy-start.3 = (f32[192,128]{1,0:T(8,128)S(1)}, f32[192,128]{1,0:T(8,128)}, u32[]{:S(2)}) copy-start(f32[192,128]{1,0:T(8,128)} %get-tuple-element.8) | copy-start | bytes 294916

commit v8 on v7

--- a/solution.py
+++ b/solution.py
@@ -672,8 +672,9 @@
             if number + 2 < len(steps):
                 scatter(1 - turb, steps[number + 2][0])
         mate_copy(dest, piece).wait_recv()
-        if number + 2 < len(steps):
+        if piece == 0 and number + 2 < len(steps):
             mate_copy(*steps[number + 2]).start()
+            mate_copy(*steps[number + 3]).start()
         start, size = pieces[piece]
         if piece == 0:
             work[dest, pl.ds(0, late), :] = grads_ref[part(turb, dest, early, late), :]

time: 78.2 us -> 78.1 us (level)
  no operation moved by 1% of the time
where the time goes in v8:
time: 78.1 us; the launch traced here: 77.9 us
  Pallas kernels  74 us (95%)
  other arithmetic  2.31 us (3%)
  local copies, waits for them, and re-layouts  0.89 us (1%)
    pallas_call x1, Pallas kernels, local_dense(): pl.pallas_call(functools.partial(step_kernel, blocks, stations, per_owner...  74 us
    add x1, other arithmetic, local_dense(): positions + moved.reshape(shape_here)  1.63 us

profile of v8, /device:TPU:0, one launch (start us, length us, event | category | flops | bytes accessed | tf_op | source)
XLA Modules:
  0.0 77.9 jit_solution(4587682927120259164)
XLA Ops:
  0.6 0.0 copy-start
  0.6 74.0 %shard_map.94 = (f32[288,128]{1,0:T(8,128)}, f32[288,128]{1,0:T(8,128)}, f32[192,128]{1,0:T(8,128)}) custom-call(s32[128]{0:T(128)} %bitcast.20, s32[128]{0:T(128)} %bitcast.22, s32[128]{0:T(128)} %bitcast.24, s32[1,128]{1,0:T(1,128)} %bitcast.21, s32[1,128]{1,0:T(1,128)} %bitcast.23, s32[1,128]{1,0:T(1,128)} %bitcast.25, f32[288,128]{1,0:T(8,128)} %bitcast.13, ...), custom_call_target="tpu_custom_call" | custom-call | tf_op jit(solution)/shard_map/pallas_call | solution.py:780
  74.7 0.0 copy-done
  74.7 0.0 copy-start.1
  74.7 0.0 copy-start.2
  74.7 1.6 %add.6 = f32[3,2,3,16,128]{4,3,2,1,0:T(8,128)} add(f32[3,2,3,16,128]{4,3,2,1,0:T(8,128)S(1)} %copy-done, f32[3,2,3,16,128]{4,3,2,1,0:T(8,128)} %bitcast.16) | non-fusion elementwise | flops 36864 | bytes 442368 | tf_op jit(solution)/shard_map/add | solution.py:824
  76.3 0.0 copy-done.1
  76.3 0.0 copy-done.2
  76.3 0.0 copy-start.3
  76.4 0.7 add.7
  77.0 0.2 copy-done.3
  77.3 0.6 copy.11
Async XLA Ops:
  0.6 74.0 %copy-start = (f32[3,2,3,16,128]{4,3,2,1,0:T(8,128)S(1)}, f32[3,2,3,16,128]{4,3,2,1,0:T(8,128)}, u32[]{:S(2)}) copy-start(f32[3,2,3,16,128]{4,3,2,1,0:T(8,128)} %param.7) | copy-start | bytes 442372
  74.7 1.7 %copy-start.1 = (f32[3,2,3,16,128]{4,3,2,1,0:T(8,128)S(1)}, f32[3,2,3,16,128]{4,3,2,1,0:T(8,128)}, u32[]{:S(2)}) copy-start(f32[3,2,3,16,128]{4,3,2,1,0:T(8,128)} %param.10) | copy-start | bytes 442372
  74.7 1.6 %copy-start.2 = (f32[288,128]{1,0:T(8,128)S(1)}, f32[288,128]{1,0:T(8,128)}, u32[]{:S(2)}) copy-start(f32[288,128]{1,0:T(8,128)} %get-tuple-element.7) | copy-start | bytes 442372
  76.3 0.9 %copy-start.3 = (f32[192,128]{1,0:T(8,128)S(1)}, f32[192,128]{1,0:T(8,128)}, u32[]{:S(2)}) copy-start(f32[192,128]{1,0:T(8,128)} %get-tuple-element.8) | copy-start | bytes 294916
